TPU v7x, 32 devices: a whole 2x2x4 slice. The times are simulated.
32 devices in a mesh: section: 2 (over x), fsdp: 16 (over z, y, core).
Axes of the slice: x: 2, y: 2, z: 4, core: 2. Of those that a mesh axis runs over, the one named last changes fastest.
Arguments:
- inputs: bfloat16 [2, 2, 2048, 2048], P(None, 'section', 'fsdp'), may hold values from -6 to 6
- top_grad: bfloat16 [2, 2048, 2048], P('section', 'fsdp'), may hold values from -6 to 6
- gains: float32 [2, 2048], P('section', 'fsdp'), may hold values from 0.25 to 1.75
- short_filters: float32 [2, 3, 7, 2048], P('section', None, None, 'fsdp'), may hold values from -2 to 2
- medium_filters: float32 [2, 128, 128], P('section', None, 'fsdp'), may hold values from -0.5 to 0.5
- lower_gain: float32 [2048], P('fsdp'), may hold values from 0.25 to 1.75
- lower_short: float32 [3, 7, 2048], P(None, None, 'fsdp'), may hold values from -2 to 2
- lower_medium: float32 [128, 128], P(None, 'fsdp'), may hold values from -0.5 to 0.5
Outputs:
- window_grads: bfloat16 [2, 2048, 2048], P('section', 'fsdp')
- gain_grads: float32 [2, 2048], P('section', 'fsdp')
- short_grads: float32 [2, 3, 7, 2048], P('section', None, None, 'fsdp')
- medium_grads: float32 [2, 128, 128], P('section', None, 'fsdp')
All inputs are finite; a program needn't handle non-finite values.
Results may differ from a plain program's by a relative error of at most 0.011.
Values may be sent and summed in bfloat16 or wider, within the bound.
A program may use at most 192 MiB of HBM per device.

v0:
```python
import jax
import jax.numpy as jnp
from jax import lax
from jax.sharding import PartitionSpec as P

TAPS = 128
SHORT = 7
CH_GROUP = 16


NORM_EPS = 1e-06


def shifted(value, axis, steps):
    count = lax.axis_size(axis)
    initial, last = (max(0, -steps), min(count, count - steps))
    return lax.ppermute(value, axis, [(source, source + steps) for source in range(initial, last)])


def from_behind(value, axis, steps):
    count = lax.axis_size(axis)
    pairs = [(source, (source + steps) % count) for source in range(count)]
    return lax.ppermute(value, axis, pairs)


def rms_scale(row_values):
    return lax.rsqrt(jnp.mean(row_values * row_values, axis=-1, keepdims=True) + NORM_EPS)


def causal_short(tap_rows, padded, length):
    running = None
    for offset in range(SHORT):
        first_row = SHORT - 1 - offset
        addend = (
            tap_rows[..., offset : offset + 1, :] * padded[..., first_row : first_row + length, :]
        )
        running = addend if running is None else running + addend
    return running


def adjoint_short(short_taps, extended, length):
    running = None
    for branch in range(3):
        for offset in range(SHORT):
            addend = short_taps[branch, offset] * extended[branch, offset : offset + length].astype(
                jnp.float32
            )
            running = addend if running is None else running + addend
    return running


def phase_split(extended, causal):
    ext_rows, channel_count = extended.shape
    copies = []
    for phase in range(4):
        if phase == 0:
            copies.append(extended)
        elif causal:
            copies.append(
                jnp.concatenate(
                    [
                        jnp.zeros((phase, channel_count), extended.dtype),
                        extended[: ext_rows - phase],
                    ],
                    0,
                )
            )
        else:
            copies.append(
                jnp.concatenate(
                    [extended[phase:], jnp.zeros((phase, channel_count), extended.dtype)], 0
                )
            )
    return jnp.stack(copies).reshape(
        4, ext_rows // TAPS, TAPS // 4, 4, channel_count // CH_GROUP, CH_GROUP
    )


def band_table(taps_b, causal):
    quarter = TAPS // 4
    upper_ids = jnp.arange(quarter)[:, None]
    lower_ids = jnp.arange(2 * quarter)[None, :]
    if causal:
        block_lag = upper_ids + quarter - lower_ids
    else:
        block_lag = lower_ids - upper_ids
    valid = (block_lag >= 0) & (block_lag < quarter)
    lag_index = 4 * jnp.clip(block_lag, 0, quarter - 1)[None] + jnp.arange(4)[:, None, None]
    values = jnp.take(taps_b, lag_index, axis=1)
    return jnp.where(valid[None, None], values, jnp.zeros_like(values))


def band_apply(table, copies):
    quarter = table.shape[2]
    result = jnp.einsum(
        "gbum,bkmvgc->kuvgc",
        table[..., :quarter],
        copies[:, :-1],
        preferred_element_type=jnp.float32,
    )
    result = result + jnp.einsum(
        "gbum,bkmvgc->kuvgc",
        table[..., quarter:],
        copies[:, 1:],
        preferred_element_type=jnp.float32,
    )
    block_count = result.shape[0]
    return result.reshape(block_count * TAPS, -1)


def lag_terms(grad_b, copies):
    quarter = TAPS // 4
    row_count, channel_count = grad_b.shape
    group_count = channel_count // CH_GROUP
    blocks = grad_b.reshape(row_count // TAPS, quarter, 4, group_count, CH_GROUP)
    first = jnp.einsum(
        "kuvgc,bkmvgc->bgum", blocks, copies[:, :-1], preferred_element_type=jnp.float32
    )
    second = jnp.einsum(
        "kuvgc,bkmvgc->bgum", blocks, copies[:, 1:], preferred_element_type=jnp.float32
    )
    full = jnp.concatenate([first, second], axis=3).reshape(4, group_count, quarter * 2 * quarter)
    full = jnp.concatenate([full, jnp.zeros((4, group_count, quarter), jnp.float32)], axis=2)
    skewed = full.reshape(4, group_count, quarter, 2 * quarter + 1).sum(axis=2)
    picked = skewed[..., 1 : quarter + 1][..., ::-1]
    return jnp.transpose(picked, (1, 2, 0)).reshape(group_count, TAPS)


def backward(cotangent, stored, params):
    own_in, own_scale, normed, query_rows, key_rows, value_rows, filtered, product_copies = stored
    gain_row, short_taps, anti_table = params
    row_count = cotangent.shape[0]
    channel_count = cotangent.shape[1]
    cot_f = cotangent.astype(jnp.float32)
    grad_filtered = (cot_f * query_rows).astype(jnp.bfloat16)
    grad_next = shifted(grad_filtered[: TAPS - 1], "fsdp", -1)
    grad_ext = jnp.concatenate(
        [grad_filtered, grad_next, jnp.zeros((1, channel_count), jnp.bfloat16)], 0
    )
    grad_product = band_apply(anti_table, phase_split(grad_ext, False))
    stacked = lax.optimization_barrier(
        jnp.stack([cot_f * filtered, grad_product * value_rows, grad_product * key_rows]).astype(
            jnp.bfloat16
        )
    )
    stacked_next = shifted(stacked[:, : SHORT - 1], "fsdp", -1)
    grad_normed = adjoint_short(short_taps, jnp.concatenate([stacked, stacked_next], 1), row_count)
    scaled = gain_row * grad_normed
    inner_mean = jnp.mean(own_in * scaled, axis=-1, keepdims=True)
    grad_in = (cot_f + own_scale * scaled - own_in * own_scale**3 * inner_mean).astype(jnp.bfloat16)
    grad_gain = jnp.sum(grad_normed * own_in * own_scale, axis=0)
    grad_short = jnp.stack(
        [
            jnp.stack(
                [
                    jnp.sum(
                        stacked[branch].astype(jnp.float32)
                        * normed[SHORT - 1 - offset : SHORT - 1 - offset + row_count],
                        axis=0,
                    )
                    for offset in range(SHORT)
                ]
            )
            for branch in range(3)
        ]
    )
    grad_medium = lag_terms(grad_filtered, product_copies)
    return (grad_in, (grad_gain, grad_short, grad_medium))


def on_device(
    inputs, top_grad, gains, short_filters, medium_filters, lower_gain, lower_short, lower_medium
):
    fsdp_size = lax.axis_size("fsdp")
    section_count = lax.axis_size("section")
    last_section = lax.axis_index("section") == section_count - 1
    gain_all, short_all, medium_all, gain_low, short_low, medium_low = (
        lax.all_gather(gains, "fsdp", axis=1, tiled=True),
        lax.all_gather(short_filters, "fsdp", axis=3, tiled=True),
        lax.all_gather(medium_filters, "fsdp", axis=2, tiled=True),
        lax.all_gather(lower_gain, "fsdp", axis=0, tiled=True),
        lax.all_gather(lower_short, "fsdp", axis=2, tiled=True),
        lax.all_gather(lower_medium, "fsdp", axis=1, tiled=True),
    )
    gain_pair = jnp.stack([gain_all[0], jnp.where(last_section, gain_low, gain_all[0])])
    short_pair = jnp.stack([short_all[0], jnp.where(last_section, short_low, short_all[0])])
    medium_pair = jnp.stack([medium_all[0], jnp.where(last_section, medium_low, medium_all[0])])
    taps_pair = medium_pair.astype(jnp.bfloat16)
    causal_tables = [band_table(taps_pair[slot_id], True) for slot_id in range(2)]
    anti_tables = [band_table(taps_pair[slot_id], False) for slot_id in range(2)]
    layer_in = inputs[:, 0]
    row_count = layer_in.shape[1]
    channel_count = layer_in.shape[2]
    behind = shifted(layer_in[:, row_count - (SHORT - 1) :], "fsdp", 1)
    padded_in = jnp.concatenate([behind, layer_in], axis=1).astype(jnp.float32)
    padded_scale = rms_scale(padded_in)
    normed = padded_in * padded_scale * gain_pair[:, None, :]
    query_rows = causal_short(short_pair[:, 0], normed, row_count)
    key_rows = causal_short(short_pair[:, 1], normed, row_count)
    value_rows = causal_short(short_pair[:, 2], normed, row_count)
    product = (key_rows * value_rows).astype(jnp.bfloat16)
    product_back = shifted(product[:, row_count - (TAPS - 1) :], "fsdp", 1)
    product_ext = jnp.concatenate(
        [jnp.zeros((2, 1, channel_count), jnp.bfloat16), product_back, product], axis=1
    )
    product_copies = [phase_split(product_ext[slot_id], True) for slot_id in range(2)]
    filtered = [band_apply(causal_tables[slot_id], product_copies[slot_id]) for slot_id in range(2)]

    def stored_for(slot_id):
        return (
            padded_in[slot_id, SHORT - 1 :],
            padded_scale[slot_id, SHORT - 1 :],
            normed[slot_id],
            query_rows[slot_id],
            key_rows[slot_id],
            value_rows[slot_id],
            filtered[slot_id],
            product_copies[slot_id],
        )

    grad_first, terms_first = backward(
        top_grad[0], stored_for(0), (gain_pair[0], short_pair[0], anti_tables[0])
    )
    second_cot = from_behind(grad_first, "section", -1)
    grad_second, terms_second = backward(
        second_cot, stored_for(1), (gain_pair[1], short_pair[1], anti_tables[1])
    )
    keep_second = jnp.where(last_section, 0.0, 1.0)
    factor = (row_count * fsdp_size) ** (-0.5)
    summed = (
        lax.psum_scatter(
            (terms_first[0] + keep_second * terms_second[0])[None],
            "fsdp",
            scatter_dimension=1,
            tiled=True,
        ),
        lax.psum_scatter(
            (terms_first[1] + keep_second * terms_second[1])[None],
            "fsdp",
            scatter_dimension=3,
            tiled=True,
        ),
        lax.psum_scatter(
            (terms_first[2] + keep_second * terms_second[2])[None],
            "fsdp",
            scatter_dimension=2,
            tiled=True,
        ),
    )
    return (grad_second[None], summed[0] * factor, summed[1] * factor, summed[2] * factor)


def solution(mesh):
    in_specs = (
        P(None, "section", "fsdp", None),
        P("section", "fsdp", None),
        P("section", "fsdp"),
        P("section", None, None, "fsdp"),
        P("section", None, "fsdp"),
        P("fsdp"),
        P(None, None, "fsdp"),
        P(None, "fsdp"),
    )
    out_specs = (
        P("section", "fsdp", None),
        P("section", "fsdp"),
        P("section", None, None, "fsdp"),
        P("section", None, "fsdp"),
    )
    return jax.shard_map(
        on_device, mesh=mesh, in_specs=in_specs, out_specs=out_specs, check_vma=False
    )
```

profile of v0, /device:TPU:1, one launch (start us, length us, event | category | flops | bytes accessed | tf_op | source)
XLA Modules:
  0.0 1331.1 jit_solution(12811569229245869453)
XLA Ops:
  13.5 20.4 %all_gather.22 = bf16[1,128,128]{1,2,0:T(8,128)(2,1)S(1)} all-gather(bf16[1,128,8]{1,2,0:T(8,128)(2,1)S(1)} %convert.453), channel_id=1, replica_groups=mesh['section'=2,'fsdp'=16] {'fsdp'}, dimensions={2}, use_global_device_ids=true | all-gather | bytes 34816 | tf_op jit(solution)/shard_map/all_gather | solution.py:180
  34.7 17.5 %all_gather.23 = bf16[128,128]{0,1:T(8,128)(2,1)S(1)} all-gather(bf16[128,8]{0,1:T(8,128)(2,1)S(1)} %convert.454), channel_id=1, replica_groups=mesh['section'=2,'fsdp'=16] {'fsdp'}, dimensions={1}, use_global_device_ids=true | all-gather | bytes 34816 | tf_op jit(solution)/shard_map/all_gather | solution.py:183
  52.2 29.2 %gather_fusion.2 = bf16[8192,128]{1,0:T(8,128)(2,1)} fusion(bf16[128,128]{0,1:T(8,128)(2,1)S(1)} %fusion.198, s32[8192]{0:T(1024)S(1)} %broadcast_clamp_fusion.1), kind=kCustom, calls=%fused_computation.2.clone | custom fusion | bytes 4227072 | tf_op jit(solution)/shard_map/jit(_take)/gather | solution.py:89
  81.4 29.2 %gather_fusion = bf16[8192,128]{1,0:T(8,128)(2,1)} fusion(bf16[128,128]{0,1:T(8,128)(2,1)S(1)} %bitcast.897, s32[8192]{0:T(1024)S(1)} %broadcast_clamp_fusion.1), kind=kCustom, calls=%fused_computation.clone | custom fusion | bytes 4227072 | tf_op jit(solution)/shard_map/jit(_take)/gather | solution.py:89
  110.7 24.0 %gather_fusion.3 = bf16[8192,128]{1,0:T(8,128)(2,1)S(1)} fusion(bf16[128,128]{0,1:T(8,128)(2,1)S(1)} %fusion.198, s32[8192]{0:T(1024)S(1)} %broadcast_clamp_fusion), kind=kCustom, calls=%fused_computation.3.clone | custom fusion | bytes 4227072 | tf_op jit(solution)/shard_map/jit(_take)/gather | solution.py:89
  134.8 29.2 %gather_fusion.1 = bf16[8192,128]{1,0:T(8,128)(2,1)} fusion(bf16[128,128]{0,1:T(8,128)(2,1)S(1)} %bitcast.898, s32[8192]{0:T(1024)S(1)} %broadcast_clamp_fusion), kind=kCustom, calls=%fused_computation.1.clone | custom fusion | bytes 4227072 | tf_op jit(solution)/shard_map/jit(_take)/gather | solution.py:89
  164.1 19.3 %all_gather.19 = f32[1,3,7,2048]{3,2,1,0:T(8,128)S(1)} all-gather(f32[1,3,7,128]{3,2,1,0:T(8,128)S(1)} %copy.109), channel_id=1, replica_groups=mesh['section'=2,'fsdp'=16] {'fsdp'}, dimensions={3}, use_global_device_ids=true | all-gather | bytes 182784 | tf_op jit(solution)/shard_map/all_gather | solution.py:179
  184.8 17.9 %all_gather.20 = f32[3,7,2048]{2,1,0:T(8,128)S(1)} all-gather(f32[3,7,128]{2,1,0:T(8,128)S(1)} %copy-done.75), channel_id=1, replica_groups=mesh['section'=2,'fsdp'=16] {'fsdp'}, dimensions={2}, use_global_device_ids=true | all-gather | bytes 182784 | tf_op jit(solution)/shard_map/all_gather | solution.py:182
  204.2 18.6 %all_gather.18 = f32[1,2048]{1,0:T(1,128)S(1)} all-gather(f32[1,128]{1,0:T(1,128)S(1)} %copy-done.83), channel_id=1, replica_groups=mesh['section'=2,'fsdp'=16] {'fsdp'}, dimensions={1}, use_global_device_ids=true | all-gather | bytes 8704 | tf_op jit(solution)/shard_map/all_gather | solution.py:178
  222.8 17.6 %all-gather = f32[16,1,128]{2,1,0:T(1,128)S(1)} all-gather(f32[1,1,128]{2,1,0:T(1,128)S(1)} %bitcast.1027), channel_id=1, replica_groups=mesh['section'=2,'fsdp'=16] {'fsdp'}, dimensions={0}, use_global_device_ids=true | all-gather | bytes 8704 | tf_op jit(solution)/shard_map/all_gather | solution.py:181
  320.5 8.3 stack.269
  328.8 16.6 %copy.119 = bf16[1,2,32,4,128,16]{2,5,0,3,4,1:T(8,128)(2,1)} copy(bf16[1,2,32,4,128,16]{5,4,3,2,1,0:T(8,128)(2,1)} %stack.269) | data formatting | bytes 2097152 | tf_op jit(solution)/shard_map/stack | solution.py:74
  346.7 8.3 stack.270
  355.0 16.6 %copy.120 = bf16[1,2,32,4,128,16]{2,5,0,3,4,1:T(8,128)(2,1)} copy(bf16[1,2,32,4,128,16]{5,4,3,2,1,0:T(8,128)(2,1)} %stack.270) | data formatting | bytes 2097152 | tf_op jit(solution)/shard_map/stack | solution.py:74
  372.9 8.3 stack.271
  381.2 16.6 %copy.121 = bf16[1,2,32,4,128,16]{2,5,0,3,4,1:T(8,128)(2,1)} copy(bf16[1,2,32,4,128,16]{5,4,3,2,1,0:T(8,128)(2,1)} %stack.271) | data formatting | bytes 2097152 | tf_op jit(solution)/shard_map/stack | solution.py:74
  397.8 16.6 %copy.118 = bf16[1,2,32,4,128,16]{2,5,0,3,4,1:T(8,128)(2,1)} copy(bf16[1,2,32,4,128,16]{5,4,3,2,1,0:T(8,128)(2,1)} %stack.268) | data formatting | bytes 2097152 | tf_op jit(solution)/shard_map/stack | solution.py:74
  414.4 15.2 %pad_maximum_fusion.1 = bf16[4,2,32,4,128,16]{2,5,0,3,4,1:T(8,128)(2,1)} fusion(bf16[1,2,32,4,128,16]{2,5,0,3,4,1:T(8,128)(2,1)} %copy.121, bf16[1,2,32,4,128,16]{2,5,0,3,4,1:T(8,128)(2,1)} %copy.120, bf16[1,2,32,4,128,16]{2,5,0,3,4,1:T(8,128)(2,1)} %copy.119, bf16[1,2,32,4,128,16]{2,5,0,3,4,1:T(8,128)(2,1)} %copy.118), kind=kLoop, calls=%fused_computation.6 | loop fusion | flops 6291456 | bytes 8388608 | tf_op jit(solution)/shard_map/stack | solution.py:74
  437.4 10.1 fusion.14
  447.5 9.0 copy.123
  475.7 8.2 stack.264
  483.9 16.8 %copy.113 = bf16[1,2,32,4,128,16]{2,5,0,3,4,1:T(8,128)(2,1)} copy(bf16[1,2,32,4,128,16]{5,4,3,2,1,0:T(8,128)(2,1)} %stack.264) | data formatting | bytes 2097152 | tf_op jit(solution)/shard_map/stack | solution.py:74
  502.2 8.2 stack.265
  510.4 16.6 %copy.114 = bf16[1,2,32,4,128,16]{2,5,0,3,4,1:T(8,128)(2,1)} copy(bf16[1,2,32,4,128,16]{5,4,3,2,1,0:T(8,128)(2,1)} %stack.265) | data formatting | bytes 2097152 | tf_op jit(solution)/shard_map/stack | solution.py:74
  528.5 8.2 stack.266
  536.7 16.7 %copy.115 = bf16[1,2,32,4,128,16]{2,5,0,3,4,1:T(8,128)(2,1)} copy(bf16[1,2,32,4,128,16]{5,4,3,2,1,0:T(8,128)(2,1)} %stack.266) | data formatting | bytes 2097152 | tf_op jit(solution)/shard_map/stack | solution.py:74
  561.6 16.6 %copy.112 = bf16[1,2,32,4,128,16]{2,5,0,3,4,1:T(8,128)(2,1)} copy(bf16[1,2,32,4,128,16]{5,4,3,2,1,0:T(8,128)(2,1)} %stack.263) | data formatting | bytes 2097152 | tf_op jit(solution)/shard_map/stack | solution.py:74
  578.2 15.5 %pad_maximum_fusion = bf16[4,2,32,4,128,16]{2,5,0,3,4,1:T(8,128)(2,1)} fusion(bf16[1,2,32,4,128,16]{2,5,0,3,4,1:T(8,128)(2,1)} %copy.115, bf16[1,2,32,4,128,16]{2,5,0,3,4,1:T(8,128)(2,1)} %copy.114, bf16[1,2,32,4,128,16]{2,5,0,3,4,1:T(8,128)(2,1)} %copy.113, bf16[1,2,32,4,128,16]{2,5,0,3,4,1:T(8,128)(2,1)} %copy.112), kind=kLoop, calls=%fused_computation.5 | loop fusion | flops 6291456 | bytes 8388608 | tf_op jit(solution)/shard_map/stack | solution.py:74
  601.4 10.2 fusion.15
  611.6 9.0 copy.117
  620.6 8.8 reshape.558
  636.1 8.5 copy.164
  652.8 8.3 fusion.19
  663.5 8.4 stack.275
  671.9 16.6 %copy.125 = bf16[1,2,32,4,128,16]{2,5,0,3,4,1:T(8,128)(2,1)} copy(bf16[1,2,32,4,128,16]{5,4,3,2,1,0:T(8,128)(2,1)} %stack.275) | data formatting | bytes 2097152 | tf_op jit(solution)/shard_map/stack | solution.py:74
  698.2 16.6 %copy.126 = bf16[1,2,32,4,128,16]{2,5,0,3,4,1:T(8,128)(2,1)} copy(bf16[1,2,32,4,128,16]{5,4,3,2,1,0:T(8,128)(2,1)} %stack.276) | data formatting | bytes 2097152 | tf_op jit(solution)/shard_map/stack | solution.py:74
  716.3 8.2 stack.277
  724.5 16.7 %copy.127 = bf16[1,2,32,4,128,16]{2,5,0,3,4,1:T(8,128)(2,1)} copy(bf16[1,2,32,4,128,16]{5,4,3,2,1,0:T(8,128)(2,1)} %stack.277) | data formatting | bytes 2097152 | tf_op jit(solution)/shard_map/stack | solution.py:74
  749.4 16.6 %copy.124 = bf16[1,2,32,4,128,16]{2,5,0,3,4,1:T(8,128)(2,1)} copy(bf16[1,2,32,4,128,16]{5,4,3,2,1,0:T(8,128)(2,1)} %stack.274) | data formatting | bytes 2097152 | tf_op jit(solution)/shard_map/stack | solution.py:74
  766.0 14.9 %pad_maximum_fusion.2 = bf16[4,2,32,4,128,16]{2,5,0,3,4,1:T(8,128)(2,1)} fusion(bf16[1,2,32,4,128,16]{2,5,0,3,4,1:T(8,128)(2,1)} %copy.127, bf16[1,2,32,4,128,16]{2,5,0,3,4,1:T(8,128)(2,1)} %copy.126, bf16[1,2,32,4,128,16]{2,5,0,3,4,1:T(8,128)(2,1)} %copy.125, bf16[1,2,32,4,128,16]{2,5,0,3,4,1:T(8,128)(2,1)} %copy.124), kind=kLoop, calls=%fused_computation.7 | loop fusion | flops 6291456 | bytes 8388608 | tf_op jit(solution)/shard_map/stack | solution.py:74
  780.9 8.8 fusion.9
  789.7 11.5 pad_maximum_fusion.4
  830.5 10.2 fusion.13
  840.7 9.0 copy.129
  849.7 8.9 reshape.564
  865.5 8.7 copy.168
  890.5 11.5 pad_maximum_fusion.5
  926.8 86.6 %all-reduce.17.cloned.1.call-done = f32[1,128,128]{1,2,0:T(8,128)} async-done(((f32[1,128,128]{1,2,0:T(8,128)}), f32[1,128,128]{1,2,0:T(8,128)}) %all-reduce.17.cloned.1.call-update) | async-done | bytes 65552
  1019.9 8.4 stack.280
  1029.6 8.3 stack.281
  1037.9 16.6 %copy.131 = bf16[1,2,32,4,128,16]{2,5,0,3,4,1:T(8,128)(2,1)} copy(bf16[1,2,32,4,128,16]{5,4,3,2,1,0:T(8,128)(2,1)} %stack.281) | data formatting | bytes 2097152 | tf_op jit(solution)/shard_map/stack | solution.py:74
  1055.8 8.3 stack.282
  1064.1 16.6 %copy.132 = bf16[1,2,32,4,128,16]{2,5,0,3,4,1:T(8,128)(2,1)} copy(bf16[1,2,32,4,128,16]{5,4,3,2,1,0:T(8,128)(2,1)} %stack.282) | data formatting | bytes 2097152 | tf_op jit(solution)/shard_map/stack | solution.py:74
  1082.0 8.3 stack.283
  1090.3 16.6 %copy.133 = bf16[1,2,32,4,128,16]{2,5,0,3,4,1:T(8,128)(2,1)} copy(bf16[1,2,32,4,128,16]{5,4,3,2,1,0:T(8,128)(2,1)} %stack.283) | data formatting | bytes 2097152 | tf_op jit(solution)/shard_map/stack | solution.py:74
  1106.9 16.6 %copy.130 = bf16[1,2,32,4,128,16]{2,5,0,3,4,1:T(8,128)(2,1)} copy(bf16[1,2,32,4,128,16]{5,4,3,2,1,0:T(8,128)(2,1)} %stack.280) | data formatting | bytes 2097152 | tf_op jit(solution)/shard_map/stack | solution.py:74
  1123.5 15.1 %pad_maximum_fusion.3 = bf16[4,2,32,4,128,16]{2,5,0,3,4,1:T(8,128)(2,1)} fusion(bf16[1,2,32,4,128,16]{2,5,0,3,4,1:T(8,128)(2,1)} %copy.133, bf16[1,2,32,4,128,16]{2,5,0,3,4,1:T(8,128)(2,1)} %copy.132, bf16[1,2,32,4,128,16]{2,5,0,3,4,1:T(8,128)(2,1)} %copy.131, bf16[1,2,32,4,128,16]{2,5,0,3,4,1:T(8,128)(2,1)} %copy.130), kind=kLoop, calls=%fused_computation.8 | loop fusion | flops 6291456 | bytes 8388608 | tf_op jit(solution)/shard_map/stack | solution.py:74
  1138.6 8.9 fusion
  1147.5 10.1 fusion.12
  1157.6 9.0 copy.135
  1184.3 13.6 %copy.182 = f32[1,3,7,2048]{0,2,1,3:T(8,128)} copy(f32[1,3,7,2048]{3,0,2,1:T(1,128)S(1)} %maximum_add_fusion) | data formatting | bytes 344064
  1205.3 15.1 %bitcast_reduce_fusion = f32[2048,3,7]{2,1,0:T(4,128)} fusion(f32[1,3,7,2048]{0,2,1,3:T(8,128)} %copy.182), kind=kLoop, calls=%fused_computation.4 | loop fusion | bytes 344064
  1228.3 33.7 %reduce-scatter.8.cloned.1.call-done = f32[128,1]{1,0:T(8,128)} async-done(((f32[2048,1]{1,0:T(8,128)}), f32[128,1]{1,0:T(8,128)}) %reduce-scatter.8.cloned.1.call-update) | async-done | bytes 528
  1263.4 58.6 %reduce-scatter.10.cloned.1.call-done = f32[128,21]{1,0:T(8,128)} async-done(((f32[2048,21]{1,0:T(8,128)}), f32[128,21]{1,0:T(8,128)}) %reduce-scatter.10.cloned.1.call-update) | async-done | bytes 10768
  (349 shorter events, 297.5 us)
Async XLA Ops:
  7.2 1006.3 %all-reduce.17.cloned.1.call-start = ((), (), s32[]{:S(2)}) async-start(), calls=%async_computation.4 | async-start | bytes 131072
  8.1 275.7 %collective-permute-start = (bf16[2,6,2048]{2,1,0:T(8,128)(2,1)S(1)}, bf16[2,6,2048]{2,1,0:T(8,128)(2,1)S(1)}, u32[]{:S(2)}, u32[]{:S(2)}) collective-permute-start(bf16[2,6,2048]{2,1,0:T(8,128)(2,1)S(1)} %slice.913), channel_id=1, source_target_pairs={{0,1},{1,2},{2,3},{3,4},{4,5},{5,6},{6,7},{7,8},{8,9},{9,10},{10,1... | collective-permute-start | bytes 147464 | tf_op jit(solution)/shard_map/ppermute | solution.py:17
  134.8 29.3 %copy-start.76 = (f32[1,3,7,128]{3,0,2,1:T(1,128)S(1)}, f32[1,3,7,128]{3,0,2,1:T(1,128)}, u32[]{:S(2)}) copy-start(f32[1,3,7,128]{3,0,2,1:T(1,128)} %param.13) | copy-start | bytes 32260
  134.8 50.0 %copy-start.75 = (f32[3,7,128]{2,1,0:T(8,128)S(1)}, f32[3,7,128]{2,1,0:T(8,128)}, u32[]{:S(2)}) copy-start(f32[3,7,128]{2,1,0:T(8,128)} %param.16) | copy-start | bytes 32260
  134.8 69.4 %copy-start.83 = (f32[1,128]{1,0:T(1,128)S(1)}, f32[1,128]{1,0:T(1,128)}, u32[]{:S(2)}) copy-start(f32[1,128]{1,0:T(1,128)} %param.12) | copy-start | bytes 1540
  134.8 88.0 %copy-start.84 = (f32[128]{0:T(128)S(1)}, f32[128]{0:T(128)}, u32[]{:S(2)}) copy-start(f32[128]{0:T(128)} %param.15) | copy-start | bytes 1540
  222.8 59.4 %copy-start.29 = (f32[1,2048]{1,0:T(1,128)}, f32[1,2048]{1,0:T(1,128)S(1)}, u32[]{:S(2)}) copy-start(f32[1,2048]{1,0:T(1,128)S(1)} %all_gather.18) | copy-start | bytes 24580
  269.5 12.7 copy-start.31
  269.6 7.0 copy-start.8
  269.6 8.8 copy-start.9
  282.3 24.8 %copy-start.79 = (bf16[256]{0:T(256)(128)(2,1)}, bf16[256]{0:T(256)(128)(2,1)S(1)}, u32[]{:S(2)}) copy-start(bf16[256]{0:T(256)(128)(2,1)S(1)} %pad.51.clone) | copy-start | bytes 1540
  284.8 9.8 copy-start
  288.9 7.5 copy-start.13
  291.2 176.0 %collective-permute-start.1 = (bf16[2,127,2048]{2,0,1:T(2,128)(2,1)}, bf16[2,127,2048]{2,0,1:T(2,128)(2,1)}, u32[]{:S(2)}, u32[]{:S(2)}) collective-permute-start(bf16[2,127,2048]{2,0,1:T(2,128)(2,1)} %copy.110), channel_id=1, source_target_pairs={{0,1},{1,2},{2,3},{3,4},{4,5},{5,6},{6,7},{7,8},{8,9},{9,10},{10,1... | collective-permute-start | bytes 3121160 | tf_op jit(solution)/shard_map/ppermute | solution.py:17
  296.4 333.0 %copy-start.10 = (f32[2,128,2048]{2,1,0:T(8,128)}, f32[2,128,2048]{2,1,0:T(8,128)S(1)}, u32[]{:S(2)}) copy-start(f32[2,128,2048]{2,1,0:T(8,128)S(1)} %multiply_add_fusion) | copy-start | bytes 6291460
  296.5 10.5 collective-permute-start.2
  414.4 15.2 %copy-start.7 = (bf16[128,4,32,64]{3,2,1,0:T(8,128)(2,1)S(1)}, bf16[128,4,32,64]{3,2,1,0:T(8,128)(2,1)}, u32[]{:S(2)}) copy-start(bf16[128,4,32,64]{3,2,1,0:T(8,128)(2,1)} %get-tuple-element.162) | copy-start | bytes 6291460
  536.7 16.7 %copy-start.20 = (bf16[1,256,2048]{2,1,0:T(8,128)(2,1)S(1)}, bf16[1,256,2048]{2,1,0:T(8,128)(2,1)}, u32[]{:S(2)}) copy-start(bf16[1,256,2048]{2,1,0:T(8,128)(2,1)} %get-tuple-element.78) | copy-start | bytes 3145732
  578.2 15.5 %copy-start.6 = (bf16[128,4,32,64]{3,2,1,0:T(8,128)(2,1)S(1)}, bf16[128,4,32,64]{3,2,1,0:T(8,128)(2,1)}, u32[]{:S(2)}) copy-start(bf16[128,4,32,64]{3,2,1,0:T(8,128)(2,1)} %get-tuple-element.160) | copy-start | bytes 6291460
  620.6 8.8 copy-start.17
  652.8 8.3 copy-start.25
  652.8 8.3 copy-start.26
  652.8 8.3 copy-start.27
  652.8 10.4 copy-start.21
  661.3 159.9 %copy-start.2 = (bf16[3,128,2048]{2,1,0:T(8,128)(2,1)}, bf16[3,128,2048]{2,1,0:T(8,128)(2,1)S(1)}, u32[]{:S(2)}) copy-start(bf16[3,128,2048]{2,1,0:T(8,128)(2,1)S(1)} %pad_maximum_fusion.7) | copy-start | bytes 4718596
  661.3 159.8 %collective-permute-start.3 = (bf16[3,6,2048]{2,1,0:T(8,128)(2,1)S(1)}, bf16[3,6,2048]{2,1,0:T(8,128)(2,1)S(1)}, u32[]{:S(2)}, u32[]{:S(2)}) collective-permute-start(bf16[3,6,2048]{2,1,0:T(8,128)(2,1)S(1)} %slice.970), channel_id=1, source_target_pairs={{1,0},{2,1},{3,2},{4,3},{5,4},{6,5},{7,6},{8,7},{9,8},{10,9},{11,1... | collective-permute-start | bytes 221192 | tf_op jit(solution)/shard_map/ppermute | solution.py:17
  724.5 16.7 %copy-start.19 = (bf16[1,256,2048]{2,1,0:T(8,128)(2,1)S(1)}, bf16[1,256,2048]{2,1,0:T(8,128)(2,1)}, u32[]{:S(2)}) copy-start(bf16[1,256,2048]{2,1,0:T(8,128)(2,1)} %get-tuple-element.77) | copy-start | bytes 3145732
  818.2 9.3 copy-start.18
  818.2 9.3 copy-start.82
  821.1 8.0 copy-start.28
  829.2 29.3 %collective-permute-start.4 = (bf16[128,2048]{1,0:T(8,128)(2,1)S(1)}, bf16[128,2048]{1,0:T(8,128)(2,1)S(1)}, u32[]{:S(2)}, u32[]{:S(2)}) collective-permute-start(bf16[128,2048]{1,0:T(8,128)(2,1)S(1)} %fusion.28), channel_id=1, source_target_pairs={{0,16},{16,0},{1,17},{17,1},{2,18},{18,2},{3,19},{19,3},{4,20},{20... | collective-permute-start | bytes 1572872 | tf_op jit(solution)/shard_map/ppermute | solution.py:23
  849.7 8.9 copy-start.11
  858.5 7.0 copy-start.22
  861.0 60.8 %copy-start.15 = (bf16[128,2048]{1,0:T(8,128)(2,1)}, bf16[128,2048]{1,0:T(8,128)(2,1)S(1)}, u32[]{:S(2)}) copy-start(bf16[128,2048]{1,0:T(8,128)(2,1)S(1)} %get-tuple-element.92) | copy-start | bytes 1572868
  918.8 5.7 copy-start.1
  921.7 93.0 %copy-start.80 = (bf16[256]{0:T(256)(128)(2,1)S(1)}, bf16[256]{0:T(256)(128)(2,1)}, u32[]{:S(2)}) copy-start(bf16[256]{0:T(256)(128)(2,1)} %copy-done.79) | copy-start | bytes 1540
  921.8 92.9 %collective-permute-start.5 = (bf16[127,2048]{1,0:T(8,128)(2,1)S(1)}, bf16[127,2048]{1,0:T(8,128)(2,1)}, u32[]{:S(2)}, u32[]{:S(2)}) collective-permute-start(bf16[127,2048]{1,0:T(8,128)(2,1)S(1)} %bitcast.914), channel_id=1, source_target_pairs={{1,0},{2,1},{3,2},{4,3},{5,4},{6,5},{7,6},{8,7},{9,8},{10,9},{11,1... | collective-permute-start | bytes 1560584 | tf_op jit(solution)/shard_map/ppermute | solution.py:17
  924.4 337.6 %reduce-scatter.8.cloned.1.call-start = ((), (), s32[]{:S(2)}) async-start(), calls=%async_computation.2 | async-start | bytes 1114112
  1181.7 16.2 %collective-permute-start.6 = (bf16[3,6,2048]{2,1,0:T(8,128)(2,1)S(1)}, bf16[3,6,2048]{2,1,0:T(8,128)(2,1)S(1)}, u32[]{:S(2)}, u32[]{:S(2)}) collective-permute-start(bf16[3,6,2048]{2,1,0:T(8,128)(2,1)S(1)} %slice.1050), channel_id=1, source_target_pairs={{1,0},{2,1},{3,2},{4,3},{5,4},{6,5},{7,6},{8,7},{9,8},{10,9},{11,1... | collective-permute-start | bytes 221192 | tf_op jit(solution)/shard_map/ppermute | solution.py:17
  1184.1 13.8 %copy-start.5 = (bf16[3,128,2048]{2,1,0:T(8,128)(2,1)S(1)}, bf16[3,128,2048]{2,1,0:T(8,128)(2,1)}, u32[]{:S(2)}) copy-start(bf16[3,128,2048]{2,1,0:T(8,128)(2,1)} %copy-done.4) | copy-start | bytes 4718596
  1184.1 13.8 %copy-start.32 = (f32[2048]{0:T(1024)S(1)}, f32[2048]{0:T(1024)}, u32[]{:S(2)}) copy-start(f32[2048]{0:T(1024)} %copy-done.31) | copy-start | bytes 24580
  1184.1 13.8 %copy-start.33 = (f32[1,1,2048]{2,1,0:T(1,128)S(1)}, f32[1,1,2048]{2,1,0:T(1,128)}, u32[]{:S(2)}) copy-start(f32[1,1,2048]{2,1,0:T(1,128)} %get-tuple-element.96) | copy-start | bytes 24580
  1184.1 13.8 %copy-start.34 = (f32[1,1,2048]{2,1,0:T(1,128)S(1)}, f32[1,1,2048]{2,1,0:T(1,128)}, u32[]{:S(2)}) copy-start(f32[1,1,2048]{2,1,0:T(1,128)} %get-tuple-element.97) | copy-start | bytes 24580
  1184.1 13.8 %copy-start.35 = (f32[1,1,2048]{2,1,0:T(1,128)S(1)}, f32[1,1,2048]{2,1,0:T(1,128)}, u32[]{:S(2)}) copy-start(f32[1,1,2048]{2,1,0:T(1,128)} %get-tuple-element.98) | copy-start | bytes 24580
  1184.1 13.8 %copy-start.36 = (f32[1,1,2048]{2,1,0:T(1,128)S(1)}, f32[1,1,2048]{2,1,0:T(1,128)}, u32[]{:S(2)}) copy-start(f32[1,1,2048]{2,1,0:T(1,128)} %get-tuple-element.99) | copy-start | bytes 24580
  1184.1 13.8 %copy-start.37 = (f32[1,1,2048]{2,1,0:T(1,128)S(1)}, f32[1,1,2048]{2,1,0:T(1,128)}, u32[]{:S(2)}) copy-start(f32[1,1,2048]{2,1,0:T(1,128)} %get-tuple-element.100) | copy-start | bytes 24580
  1184.1 13.8 %copy-start.38 = (f32[1,1,2048]{2,1,0:T(1,128)S(1)}, f32[1,1,2048]{2,1,0:T(1,128)}, u32[]{:S(2)}) copy-start(f32[1,1,2048]{2,1,0:T(1,128)} %get-tuple-element.101) | copy-start | bytes 24580
  1184.1 13.8 %copy-start.39 = (f32[1,1,2048]{2,1,0:T(1,128)S(1)}, f32[1,1,2048]{2,1,0:T(1,128)}, u32[]{:S(2)}) copy-start(f32[1,1,2048]{2,1,0:T(1,128)} %get-tuple-element.102) | copy-start | bytes 24580
  1184.1 13.8 %copy-start.40 = (f32[1,1,2048]{2,1,0:T(1,128)S(1)}, f32[1,1,2048]{2,1,0:T(1,128)}, u32[]{:S(2)}) copy-start(f32[1,1,2048]{2,1,0:T(1,128)} %get-tuple-element.103) | copy-start | bytes 24580
  1184.2 13.8 %copy-start.41 = (f32[1,1,2048]{2,1,0:T(1,128)S(1)}, f32[1,1,2048]{2,1,0:T(1,128)}, u32[]{:S(2)}) copy-start(f32[1,1,2048]{2,1,0:T(1,128)} %get-tuple-element.104) | copy-start | bytes 24580
  1184.2 13.8 %copy-start.42 = (f32[1,1,2048]{2,1,0:T(1,128)S(1)}, f32[1,1,2048]{2,1,0:T(1,128)}, u32[]{:S(2)}) copy-start(f32[1,1,2048]{2,1,0:T(1,128)} %get-tuple-element.105) | copy-start | bytes 24580
  1184.2 13.8 %copy-start.43 = (f32[1,1,2048]{2,1,0:T(1,128)S(1)}, f32[1,1,2048]{2,1,0:T(1,128)}, u32[]{:S(2)}) copy-start(f32[1,1,2048]{2,1,0:T(1,128)} %get-tuple-element.106) | copy-start | bytes 24580
  1184.2 13.8 %copy-start.44 = (f32[1,1,2048]{2,1,0:T(1,128)S(1)}, f32[1,1,2048]{2,1,0:T(1,128)}, u32[]{:S(2)}) copy-start(f32[1,1,2048]{2,1,0:T(1,128)} %get-tuple-element.107) | copy-start | bytes 24580
  1184.2 13.8 %copy-start.45 = (f32[1,1,2048]{2,1,0:T(1,128)S(1)}, f32[1,1,2048]{2,1,0:T(1,128)}, u32[]{:S(2)}) copy-start(f32[1,1,2048]{2,1,0:T(1,128)} %get-tuple-element.108) | copy-start | bytes 24580
  1184.2 13.8 %copy-start.46 = (f32[1,1,2048]{2,1,0:T(1,128)S(1)}, f32[1,1,2048]{2,1,0:T(1,128)}, u32[]{:S(2)}) copy-start(f32[1,1,2048]{2,1,0:T(1,128)} %get-tuple-element.109) | copy-start | bytes 24580
  1184.2 13.8 %copy-start.47 = (f32[1,1,2048]{2,1,0:T(1,128)S(1)}, f32[1,1,2048]{2,1,0:T(1,128)}, u32[]{:S(2)}) copy-start(f32[1,1,2048]{2,1,0:T(1,128)} %get-tuple-element.110) | copy-start | bytes 24580
  1184.2 13.8 %copy-start.48 = (f32[1,1,2048]{2,1,0:T(1,128)S(1)}, f32[1,1,2048]{2,1,0:T(1,128)}, u32[]{:S(2)}) copy-start(f32[1,1,2048]{2,1,0:T(1,128)} %get-tuple-element.111) | copy-start | bytes 24580
  1184.2 13.8 %copy-start.49 = (f32[1,1,2048]{2,1,0:T(1,128)S(1)}, f32[1,1,2048]{2,1,0:T(1,128)}, u32[]{:S(2)}) copy-start(f32[1,1,2048]{2,1,0:T(1,128)} %get-tuple-element.112) | copy-start | bytes 24580
  1184.2 13.8 %copy-start.50 = (f32[1,1,2048]{2,1,0:T(1,128)S(1)}, f32[1,1,2048]{2,1,0:T(1,128)}, u32[]{:S(2)}) copy-start(f32[1,1,2048]{2,1,0:T(1,128)} %get-tuple-element.113) | copy-start | bytes 24580
  1184.3 13.8 %copy-start.51 = (f32[1,1,2048]{2,1,0:T(1,128)S(1)}, f32[1,1,2048]{2,1,0:T(1,128)}, u32[]{:S(2)}) copy-start(f32[1,1,2048]{2,1,0:T(1,128)} %get-tuple-element.114) | copy-start | bytes 24580
  1184.3 13.8 %copy-start.71 = (f32[1,1,2048]{2,1,0:T(1,128)S(1)}, f32[1,1,2048]{2,1,0:T(1,128)}, u32[]{:S(2)}) copy-start(f32[1,1,2048]{2,1,0:T(1,128)} %get-tuple-element.115) | copy-start | bytes 24580
  1184.3 13.8 %copy-start.72 = (f32[1,1,2048]{2,1,0:T(1,128)S(1)}, f32[1,1,2048]{2,1,0:T(1,128)}, u32[]{:S(2)}) copy-start(f32[1,1,2048]{2,1,0:T(1,128)} %get-tuple-element.116) | copy-start | bytes 24580
  1184.3 13.8 %copy-start.77 = (f32[128]{0:T(128)S(1)}, f32[128]{0:T(128)}, u32[]{:S(2)}) copy-start(f32[128]{0:T(128)} %get-tuple-element.166) | copy-start | bytes 1540
  1205.2 116.9 %reduce-scatter.10.cloned.1.call-start = ((), (), s32[]{:S(2)}) async-start(), calls=%async_computation.3 | async-start | bytes 1114112
  (33 other events, 113.0 us)
Sparse Core Ops, SparseCore 0:
  924.5 88.8 all-reduce.16
  1205.3 56.6 reduce-scatter.7
  1265.6 56.3 reduce-scatter.9
where the time goes:
time: 1340 us; the launch traced here: 1330 us
  local copies, waits for them, and re-layouts  746 us (56%)
  waiting for transfers between devices  184 us (14%)
  other arithmetic  149 us (11%)
  blocking collectives  111 us (8%)
  matrix products  106 us (8%)
  starting transfers between devices  17.7 us (1%)
  between operations  16.4 us (1%)
    another operation x32, local copies, waits for them, and re-layouts, phase_split(): jnp.stack(copies)  398 us
    unnamed x6, waiting for transfers between devices  179 us
    gather x8, local copies, waits for them, and re-layouts, band_table(): values = jnp.take(taps_b, lag_index, axis=1)  140 us
    another operation x4, other arithmetic, phase_split(): jnp.stack(copies)  60.6 us
    unnamed x201, local copies, waits for them, and re-layouts  53.1 us
    dot_general x4, matrix products, band_apply(): jnp.einsum('gbum,bkmvgc->kuvgc', table[..., quarter:], copies[:, 1:], pre...  37 us
    dot_general x4, matrix products, band_apply(): jnp.einsum('gbum,bkmvgc->kuvgc', table[..., :quarter], copies[:, :-1], pr...  36.8 us
    add x4, local copies, waits for them, and re-layouts, band_apply(): result + jnp.einsum('gbum,bkmvgc->kuvgc', table[..., quarter:], copies[:,...  36 us
  transfers between devices with their start and end apart: 10, of which 4 were waited for; matrix products, arithmetic and copies ran while one was open for 41% of the time, Pallas kernels for 0%

commit v1 on v0

v1 whole, which is shorter than its diff:
```python
import jax
import jax.numpy as jnp
from jax import lax
from jax.experimental import pallas as pl
from jax.experimental.pallas import tpu as pltpu
from jax.sharding import PartitionSpec as P

TAPS = 128
SHORT = 7
CH_GROUP = 16
NORM_EPS = 1e-06
LANES = 128
PER = LANES // CH_GROUP
EDGE = 16
F32 = jnp.float32
BF16 = jnp.bfloat16
PARAMS = dict(vmem_limit_bytes=48 * 2**20)


def toeplitz(row, rows):
    wide = jnp.broadcast_to(row, (rows, 2 * TAPS))
    return pltpu.roll(wide, 0, 1, stride=1, stride_axis=0).astype(BF16)


def band(table_ref, signal_ref):
    head = signal_ref[: 2 * TAPS]
    tail = signal_ref[TAPS : 3 * TAPS]
    group = lax.broadcasted_iota(jnp.int32, (TAPS, LANES), 1) // CH_GROUP
    group_edge = lax.broadcasted_iota(jnp.int32, (EDGE, LANES), 1) // CH_GROUP
    main = jnp.zeros((TAPS, LANES), F32)
    edge = jnp.zeros((EDGE, LANES), F32)
    edges = []
    for g in range(PER):
        table = toeplitz(table_ref[g : g + 1, :], TAPS)
        edges.append(table[:EDGE])
        part = jnp.dot(table, head, preferred_element_type=F32)
        main = jnp.where(group == g, part, main)
    parts = jnp.dot(jnp.concatenate(edges, 0), tail, preferred_element_type=F32)
    for g in range(PER):
        edge = jnp.where(group_edge == g, parts[g * EDGE : (g + 1) * EDGE], edge)
    return main, edge


def forward_kernel(
    x_ref, r_ref, gain_ref, short_ref, table_ref, q_ref, k_ref, v_ref, u_ref, w_ref, g_ref, us, ws
):
    total = x_ref.shape[0]
    own = TAPS + EDGE
    us[...] = x_ref[...].astype(F32) * r_ref[...] * gain_ref[...]
    u_ref[...] = us[TAPS : TAPS + own]
    half = (2 * TAPS + EDGE) // 2
    for part in range(2):
        low = part * half
        acc = None
        for j in range(SHORT):
            add = short_ref[j : j + 1, :] * us[own + low - j : own + low - j + half]
            acc = add if acc is None else acc + add
        q_ref[low : low + half] = acc
    for low, size in ((0, TAPS), (TAPS, own)):
        keys, values = None, None
        for j in range(SHORT):
            rows = us[EDGE + low - j : EDGE + low - j + size]
            key = short_ref[SHORT + j : SHORT + j + 1, :] * rows
            value = short_ref[2 * SHORT + j : 2 * SHORT + j + 1, :] * rows
            keys = key if keys is None else keys + key
            values = value if values is None else values + value
        ws[low : low + size] = (keys * values).astype(BF16)
        if low:
            k_ref[...] = keys
            v_ref[...] = values
    ws[2 * TAPS + EDGE :] = jnp.zeros((TAPS - EDGE, LANES), BF16)
    w_ref[...] = ws[: 2 * TAPS]
    main, edge = band(table_ref, ws)
    g_ref[:TAPS] = main
    g_ref[TAPS:] = edge


def backward_kernel(
    e_ref, q_ref, k_ref, v_ref, g_ref, xf_ref, x_ref, r_ref, gain_ref, short_ref, table_ref,
    dx_ref, dg_ref, da_ref, du_ref, dgs, das, held, means,
):
    step = pl.program_id(0)
    steps = pl.num_programs(0)
    own = TAPS + EDGE
    dgs[: TAPS + own] = (e_ref[...].astype(F32) * q_ref[...]).astype(BF16)
    dgs[TAPS + own :] = jnp.zeros((TAPS - EDGE, LANES), BF16)
    dg_ref[...] = dgs[:TAPS]
    main, edge = band(table_ref, dgs)
    for low, size, dw in ((0, TAPS, main), (TAPS, EDGE, edge)):
        rows = slice(low, low + size)
        das[0, rows] = (e_ref[rows].astype(F32) * g_ref[rows]).astype(BF16).astype(F32)
        das[1, rows] = (dw * v_ref[rows]).astype(BF16).astype(F32)
        das[2, rows] = (dw * k_ref[rows]).astype(BF16).astype(F32)
    da_ref[...] = das[:, :TAPS].astype(BF16)
    acc = None
    for c in range(3):
        for j in range(SHORT):
            add = short_ref[SHORT * c + j : SHORT * c + j + 1, :] * das[c, j : j + TAPS]
            acc = add if acc is None else acc + add
    du_ref[...] = acc
    scaled = gain_ref[...] * acc
    part = jnp.sum(x_ref[...].astype(F32) * scaled, axis=1, keepdims=True)

    @pl.when(step == 0)
    def _():
        means[...] = jnp.zeros_like(means)

    means[...] += part
    held[step] = e_ref[:TAPS].astype(F32) + r_ref[...] * scaled

    @pl.when(step == steps - 1)
    def _():
        r = r_ref[...]
        factor = r * r * r * (means[...] * (1.0 / dx_ref.shape[1]))
        for b in range(dx_ref.shape[1] // LANES):
            lanes = slice(b * LANES, (b + 1) * LANES)
            dx_ref[:, lanes] = (held[b] - xf_ref[:, lanes].astype(F32) * factor).astype(BF16)


def terms_kernel(
    dg_ref, da_ref, du_ref, u_ref, w_ref, x_ref, r_ref, tg_ref, ts_ref, tm_ref
):
    tg_ref[...] = jnp.sum(du_ref[...] * x_ref[...].astype(F32) * r_ref[...], axis=0, keepdims=True)
    for c in range(3):
        grads = da_ref[c].astype(F32)
        for j in range(SHORT):
            row = SHORT * c + j
            ts_ref[row : row + 1, :] = jnp.sum(
                grads * u_ref[EDGE - j : EDGE - j + TAPS], axis=0, keepdims=True
            )
    ts_ref[3 * SHORT :, :] = jnp.zeros((3, LANES), F32)
    grads = dg_ref[...].astype(F32)
    mask = (
        lax.broadcasted_iota(jnp.int32, (1, PER, LANES), 2) // CH_GROUP
        == lax.broadcasted_iota(jnp.int32, (1, PER, LANES), 1)
    )
    spread = jnp.where(mask, jnp.broadcast_to(grads[:, None, :], (TAPS, PER, LANES)), 0.0)
    spread = spread.reshape(TAPS * PER, LANES).astype(BF16)
    lags = lax.dot_general(
        spread, w_ref[...], (((1,), (1,)), ((), ())), preferred_element_type=F32
    )
    total = lags[:PER]
    for t in range(1, TAPS):
        total = total + pltpu.roll(lags[t * PER : (t + 1) * PER], 2 * TAPS - t, 1)
    tm_ref[...] = total


def tall(rows, dtype=F32):
    return pl.BlockSpec((rows, LANES), lambda i: (0, i))


def whole(shape):
    return pl.BlockSpec(shape, lambda i: (0,) * len(shape))


GROUP_SPEC = pl.BlockSpec((PER, 2 * TAPS), lambda i: (i, 0))
BRANCH_SPEC = pl.BlockSpec((3, TAPS, LANES), lambda i: (0, 0, i))


def run_forward(x_ext, r_ext, gain, short, table):
    total, channels = x_ext.shape
    own = TAPS + EDGE
    shapes = [
        ((TAPS + own), F32), (own, F32), (own, F32), (own, F32), (2 * TAPS, BF16), (own, F32),
    ]
    return pl.pallas_call(
        forward_kernel,
        grid=(channels // LANES,),
        in_specs=[tall(total), whole((total, 1)), tall(1), tall(24), GROUP_SPEC],
        out_specs=[tall(rows) for rows, _ in shapes],
        out_shape=[jax.ShapeDtypeStruct((rows, channels), kind) for rows, kind in shapes],
        scratch_shapes=[pltpu.VMEM((total, LANES), F32), pltpu.VMEM((3 * TAPS, LANES), BF16)],
        compiler_params=pltpu.CompilerParams(**PARAMS),
        cost_estimate=pl.CostEstimate(flops=4 * 10**9, bytes_accessed=12 * 10**6, transcendentals=0),
    )(x_ext, r_ext, gain, short, table)


def run_backward(e_ext, q, k, v, g, x, r, gain, short, table):
    channels = x.shape[1]
    own = TAPS + EDGE
    blocks = channels // LANES
    return pl.pallas_call(
        backward_kernel,
        grid=(blocks,),
        in_specs=[
            tall(TAPS + own), tall(TAPS + own), tall(own), tall(own), tall(own),
            whole((TAPS, channels)), tall(TAPS), whole((TAPS, 1)), tall(1), tall(24), GROUP_SPEC,
        ],
        out_specs=[whole((TAPS, channels)), tall(TAPS), BRANCH_SPEC, tall(TAPS)],
        out_shape=[
            jax.ShapeDtypeStruct((TAPS, channels), BF16),
            jax.ShapeDtypeStruct((TAPS, channels), BF16),
            jax.ShapeDtypeStruct((3, TAPS, channels), BF16),
            jax.ShapeDtypeStruct((TAPS, channels), F32),
        ],
        scratch_shapes=[
            pltpu.VMEM((3 * TAPS, LANES), BF16),
            pltpu.VMEM((3, own, LANES), F32),
            pltpu.VMEM((blocks, TAPS, LANES), F32),
            pltpu.VMEM((TAPS, 1), F32),
        ],
        compiler_params=pltpu.CompilerParams(**PARAMS),
        cost_estimate=pl.CostEstimate(flops=4 * 10**9, bytes_accessed=12 * 10**6, transcendentals=0),
    )(e_ext, q, k, v, g, x, x, r, gain, short, table)


def run_terms(dg, da, du, u, w, x, r):
    channels = x.shape[1]
    return pl.pallas_call(
        terms_kernel,
        grid=(channels // LANES,),
        in_specs=[
            tall(TAPS), BRANCH_SPEC, tall(TAPS), tall(TAPS + EDGE), tall(2 * TAPS), tall(TAPS),
            whole((TAPS, 1)),
        ],
        out_specs=[tall(1), tall(24), GROUP_SPEC],
        out_shape=[
            jax.ShapeDtypeStruct((1, channels), F32),
            jax.ShapeDtypeStruct((24, channels), F32),
            jax.ShapeDtypeStruct((channels // CH_GROUP, 2 * TAPS), F32),
        ],
        compiler_params=pltpu.CompilerParams(**PARAMS),
        cost_estimate=pl.CostEstimate(flops=4 * 10**9, bytes_accessed=8 * 10**6, transcendentals=0),
    )(dg, da, du, u, w, x, r)


def shifted(value, steps):
    count = lax.axis_size("fsdp")
    initial, last = (max(0, -steps), min(count, count - steps))
    return lax.ppermute(value, "fsdp", [(source, source + steps) for source in range(initial, last)])


def crossed(value, steps):
    sections, count = lax.axis_size("section"), lax.axis_size("fsdp")
    pairs = [
        (s * count + f, ((s - 1) % sections) * count + f - steps)
        for s in range(sections)
        for f in range(steps, count)
    ]
    return lax.ppermute(value, ("section", "fsdp"), pairs)


def on_device(
    inputs, top_grad, gains, short_filters, medium_filters, lower_gain, lower_short, lower_medium
):
    shards = lax.axis_size("fsdp")
    last_section = lax.axis_index("section") == lax.axis_size("section") - 1
    chunk = gains.shape[1]
    channels = chunk * shards
    flat = jnp.stack(
        [
            jnp.concatenate([gains.reshape(-1), short_filters.reshape(-1), medium_filters.reshape(-1)]),
            jnp.concatenate([lower_gain, lower_short.reshape(-1), lower_medium.reshape(-1)]),
        ]
    )
    every = lax.all_gather(flat, "fsdp", axis=0, tiled=False)

    def layer_params(part):
        gain = part[:, :chunk].reshape(1, channels)
        short = jnp.transpose(
            part[:, chunk : 22 * chunk].reshape(shards, 3 * SHORT, chunk), (1, 0, 2)
        ).reshape(3 * SHORT, channels)
        medium = jnp.transpose(
            part[:, 22 * chunk :].reshape(shards, -1, TAPS // shards), (1, 0, 2)
        ).reshape(-1, TAPS)
        medium = medium.astype(BF16).astype(F32)
        short = jnp.pad(short, ((0, 3), (0, 0)))
        causal = jnp.pad(medium[:, ::-1], ((0, 0), (1, TAPS - 1)))
        anti = jnp.pad(medium, ((0, 0), (0, TAPS)))
        return gain, short, causal, anti

    upper = every[:, 0]
    params = (layer_params(upper), layer_params(jnp.where(last_section, every[:, 1], upper)))

    def extended(x):
        rows = x.shape[0]
        x_ext = jnp.concatenate(
            [
                shifted(x[rows - EDGE :], 2), shifted(x, 1), x, shifted(x, -1),
                shifted(x[:EDGE], -2),
            ]
        )
        wide = x_ext.astype(F32)
        r_ext = lax.rsqrt(jnp.mean(wide * wide, axis=-1, keepdims=True) + NORM_EPS)
        return x_ext, r_ext

    def terms_of(x, r, ahead, back):
        return run_terms(back[1], back[2], back[3], ahead[3], ahead[4], x, r)

    x1, x2, e1 = inputs[0, 0], inputs[1, 0], top_grad[0]
    e1_ext = jnp.concatenate([e1, shifted(e1, -1), shifted(e1[:EDGE], -2)])
    x1_ext, r1_ext = extended(x1)
    x2_ext, r2_ext = extended(x2)
    own_rows = slice(TAPS + EDGE, 2 * TAPS + EDGE)
    r1, r2 = r1_ext[own_rows], r2_ext[own_rows]
    (gain1, short1, causal1, anti1), (gain2, short2, causal2, anti2) = params
    ahead1 = run_forward(x1_ext, r1_ext, gain1, short1, causal1)
    back1 = run_backward(
        e1_ext, ahead1[0], ahead1[1], ahead1[2], ahead1[5], x1, r1, gain1, short1, anti1
    )
    dx1 = back1[0]
    e2_ext = jnp.concatenate([crossed(dx1, 0), crossed(dx1, 1), crossed(dx1[:EDGE], 2)])
    ahead2 = run_forward(x2_ext, r2_ext, gain2, short2, causal2)
    terms1 = terms_of(x1, r1, ahead1, back1)
    back2 = run_backward(
        e2_ext, ahead2[0], ahead2[1], ahead2[2], ahead2[5], x2, r2, gain2, short2, anti2
    )
    terms2 = terms_of(x2, r2, ahead2, back2)
    keep = jnp.where(last_section, 0.0, 1.0)
    tg, ts, tm = [a + keep * b for a, b in zip(terms1, terms2)]
    ts = jnp.transpose(ts[: 3 * SHORT].reshape(3 * SHORT, shards, chunk), (1, 0, 2))
    tm = tm[:, 1 : TAPS + 1][:, ::-1]
    groups = tm.shape[0]
    tm = jnp.transpose(tm.reshape(groups, shards, TAPS // shards), (1, 0, 2))
    packed = jnp.concatenate(
        [tg.reshape(shards, chunk), ts.reshape(shards, -1), tm.reshape(shards, -1)], axis=1
    )
    factor = (x1.shape[0] * shards) ** (-0.5)
    width = packed.shape[1]
    room = -(-width // 1024) * 1024
    packed = jnp.pad(packed, ((0, 0), (0, room - width))).reshape(shards * room)
    summed = lax.psum_scatter(packed, "fsdp", scatter_dimension=0, tiled=True) * factor
    return (
        back2[0][None],
        summed[:chunk][None],
        summed[chunk : 22 * chunk].reshape(1, 3, SHORT, chunk),
        summed[22 * chunk : 30 * chunk].reshape(1, groups, TAPS // shards),
    )


def solution(mesh):
    in_specs = (
        P(None, "section", "fsdp", None),
        P("section", "fsdp", None),
        P("section", "fsdp"),
        P("section", None, None, "fsdp"),
        P("section", None, "fsdp"),
        P("fsdp"),
        P(None, None, "fsdp"),
        P(None, "fsdp"),
    )
    out_specs = (
        P("section", "fsdp", None),
        P("section", "fsdp"),
        P("section", None, None, "fsdp"),
        P("section", None, "fsdp"),
    )
    return jax.shard_map(
        on_device, mesh=mesh, in_specs=in_specs, out_specs=out_specs, check_vma=False
    )
```

time: 1340 us -> 291 us (0.22)
  local copies, waits for them, and re-layouts: 746 us -> 27.9 us
  other arithmetic: 149 us -> 4.33 us
  matrix products: 106 us -> 0 us
  blocking collectives: 111 us -> 23.9 us
  waiting for transfers between devices: 184 us -> 97 us
  Pallas kernels: 0 us -> 85 us
  starting transfers between devices: 17.7 us -> 34.1 us
    another operation x46 -> x2, local copies, waits for them, and re-layouts: 412 us -> 0.03 us  [on_device(): jnp.stack([jnp.concatenate([gains.reshape(-1), short_filters.reshape(-1),...]
    gather x8 -> x0, local copies, waits for them, and re-layouts: 140 us -> none  [band_table(): values = jnp.take(taps_b, lag_index, axis=1)]
    dot_general x12 -> x0, matrix products: 106 us -> none  [the longest x4 37 us: band_apply(): jnp.einsum('gbum,bkmvgc->kuvgc', table[..., quarter:], copies[:, 1:], pre...]
    all_gather x6 -> x1, blocking collectives: 111 us -> 23.9 us  [on_device(): every = lax.all_gather(flat, 'fsdp', axis=0, tiled=False)]
    pallas_call x0 -> x6, Pallas kernels: none -> 85 us  [the longest x2 30.7 us: run_backward(): pl.pallas_call(backward_kernel, grid=(blocks,), in_specs=[tall(TAPS + own...]
    unnamed x6 -> x2, waiting for transfers between devices: 179 us -> 95.7 us
    another operation x10 -> x0, other arithmetic: 68.1 us -> none  [the longest x4 60.6 us: phase_split(): jnp.stack(copies)]
    add x4 -> x0, local copies, waits for them, and re-layouts: 36 us -> none  [band_apply(): result + jnp.einsum('gbum,bkmvgc->kuvgc', table[..., quarter:], copies[:,...]
  transfers between devices with their start and end apart: 10 -> 14, of which waited for: 4 -> 2; matrix products, arithmetic and copies ran while one was open for 41% -> 4% of each run, Pallas kernels for 0% -> 20%
where the time goes in v1:
time: 291 us; the launch traced here: 288 us
  waiting for transfers between devices  97 us (33%)
  Pallas kernels  85 us (29%)
  starting transfers between devices  34.1 us (12%)
  local copies, waits for them, and re-layouts  27.9 us (10%)
  blocking collectives  23.9 us (8%)
  between operations  15.6 us (5%)
  other arithmetic  4.33 us (1%)
    unnamed x2, waiting for transfers between devices  95.7 us
    pallas_call x2, Pallas kernels, run_backward(): pl.pallas_call(backward_kernel, grid=(blocks,), in_specs=[tall(TAPS + own...  30.7 us
    pallas_call x2, Pallas kernels, run_forward(): pl.pallas_call(forward_kernel, grid=(channels // LANES,), in_specs=[tall(...  28.4 us
    ppermute x10, starting transfers between devices, shifted(): lax.ppermute(value, 'fsdp', [(source, source + steps) for source in range...  28.3 us
    pallas_call x2, Pallas kernels, run_terms(): pl.pallas_call(terms_kernel, grid=(channels // LANES,), in_specs=[tall(TA...  25.9 us
    all_gather x1, blocking collectives, on_device(): every = lax.all_gather(flat, 'fsdp', axis=0, tiled=False)  23.9 us
    unnamed x81, local copies, waits for them, and re-layouts  19.8 us
  transfers between devices with their start and end apart: 14, of which 2 were waited for; matrix products, arithmetic and copies ran while one was open for 4% of the time, Pallas kernels for 20%

profile of v1, /device:TPU:1, one launch (start us, length us, event | category | flops | bytes accessed | tf_op | source)
XLA Modules:
  0.0 287.8 jit_solution(14147553379184378145)
XLA Ops:
  7.3 1.3 slice_bitcast_fusion
  8.6 2.0 collective-permute-start.11
  10.6 4.5 %collective-permute-start.10 = (bf16[128,2048]{1,0:T(8,128)(2,1)S(1)}, bf16[128,2048]{1,0:T(8,128)(2,1)}, u32[]{:S(2)}, u32[]{:S(2)}) collective-permute-start(bf16[128,2048]{1,0:T(8,128)(2,1)S(1)} %get-tuple-element.74.xf_ref.x_ref), channel_id=1, source_target_pairs={{0,1},{1,2},{2,3},{3,4},{4,5},{5,6},{6,7},{7,8},{8,9},{9,10},{10,1... | collective-permute-start | bytes 1572872 | tf_op jit(solution)/shard_map/ppermute | solution.py:230
  15.1 1.9 collective-permute-start.4
  17.0 3.6 %collective-permute-start.3 = (bf16[128,2048]{1,0:T(8,128)(2,1)S(1)}, bf16[128,2048]{1,0:T(8,128)(2,1)}, u32[]{:S(2)}, u32[]{:S(2)}) collective-permute-start(bf16[128,2048]{1,0:T(8,128)(2,1)S(1)} %get-tuple-element.75.xf_ref.x_ref), channel_id=1, source_target_pairs={{0,1},{1,2},{2,3},{3,4},{4,5},{5,6},{6,7},{7,8},{8,9},{9,10},{10,1... | collective-permute-start | bytes 1572872 | tf_op jit(solution)/shard_map/ppermute | solution.py:230
  20.7 1.6 slice_bitcast_fusion.2
  22.3 4.9 %collective-permute-start.2 = (bf16[16,2048]{1,0:T(8,128)(2,1)}, bf16[16,2048]{1,0:T(8,128)(2,1)S(1)}, u32[]{:S(2)}, u32[]{:S(2)}) collective-permute-start(bf16[16,2048]{1,0:T(8,128)(2,1)} %get-tuple-element.71), channel_id=1, source_target_pairs={{0,2},{1,3},{2,4},{3,5},{4,6},{5,7},{6,8},{7,9},{8,10},{9,11},{10,... | collective-permute-start | bytes 196616 | tf_op jit(solution)/shard_map/ppermute | solution.py:230
  27.8 23.9 %all-gather.1 = f32[16,2,3840]{2,1,0:T(2,128)S(1)} all-gather(f32[1,2,3840]{2,1,0:T(2,128)S(1)} %maximum_bitcast_fusion), channel_id=2, replica_groups=mesh['section'=2,'fsdp'=16] {'fsdp'}, dimensions={0}, use_global_device_ids=true | all-gather | bytes 522240 | tf_op jit(solution)/shard_map/all_gather | solution.py:256
  51.7 0.4 fusion.4
  52.2 0.2 copy.78
  52.4 0.2 copy.79
  52.6 0.1 copy.80
  52.8 0.2 copy.70
  53.0 0.2 copy.71
  53.7 0.5 slice-done
  54.6 4.6 %collective-permute-start.9 = (bf16[16,2048]{1,0:T(8,128)(2,1)S(1)}, bf16[16,2048]{1,0:T(8,128)(2,1)S(1)}, u32[]{:S(2)}, u32[]{:S(2)}) collective-permute-start(bf16[16,2048]{1,0:T(8,128)(2,1)S(1)} %get-tuple-element.69), channel_id=1, source_target_pairs={{0,2},{1,3},{2,4},{3,5},{4,6},{5,7},{6,8},{7,9},{8,10},{9,11},{10,... | collective-permute-start | bytes 196616 | tf_op jit(solution)/shard_map/ppermute | solution.py:230
  59.3 1.3 collective-permute-done.9
  60.6 1.3 collective-permute-start.1
  61.9 1.3 collective-permute-start.12
  63.2 1.1 constant_dynamic-update-slice_fusion.3
  64.3 1.3 collective-permute-start.5
  65.6 1.1 constant_dynamic-update-slice_fusion.8
  66.8 1.2 copy-done.18
  68.0 2.9 %collective-permute-start = (bf16[128,2048]{1,0:T(8,128)(2,1)S(1)}, bf16[128,2048]{1,0:T(8,128)(2,1)}, u32[]{:S(2)}, u32[]{:S(2)}) collective-permute-start(bf16[128,2048]{1,0:T(8,128)(2,1)S(1)} %bitcast.96), channel_id=1, source_target_pairs={{1,0},{2,1},{3,2},{4,3},{5,4},{6,5},{7,6},{8,7},{9,8},{10,9},{11,1... | collective-permute-start | bytes 1572872 | tf_op jit(solution)/shard_map/ppermute | solution.py:230
  70.9 1.1 constant_dynamic-update-slice_fusion.1
  72.0 0.4 multiply_reduce_fusion.1
  72.4 0.8 copy-done.21
  73.2 0.1 copy.73.r_ref
  73.3 14.1 %shard_map.111 = (f32[272,2048]{1,0:T(8,128)}, f32[144,2048]{1,0:T(8,128)S(1)}, f32[144,2048]{1,0:T(8,128)S(1)}, f32[144,2048]{1,0:T(8,128)S(1)}, bf16[256,2048]{1,0:T(8,128)(2,1)S(1)}, /*index=5*/f32[144,2048]{1,0:T(8,128)}) custom-call(bf16[416,2048]{1,0:T(8,128)(2,1)} %copy-done.21, f32[416,1]{1,0:T(8,128)S(1)} %copy.73.r_ref, f32[1,2048]{1,0:T(1,128)S(1)} %bitcast.77, ...), custom_call_target="tpu_custom_call" | custom-call | flops 4000000000 | bytes 12000000 | tf_op jit(solution)/shard_map/pallas_call | solution.py:166
  87.4 1.1 copy-done.4
  88.5 1.1 copy-done.6
  89.6 1.0 copy-done.9
  90.6 1.0 copy-done.13
  91.7 0.1 copy.75.r_ref
  91.8 1.2 pad_maximum_fusion.e_ref
  93.0 0.2 copy-done.5
  93.2 15.4 %shard_map.112 = (bf16[128,2048]{1,0:T(8,128)(2,1)S(1)}, bf16[128,2048]{1,0:T(8,128)(2,1)S(1)}, bf16[3,128,2048]{2,1,0:T(8,128)(2,1)}, f32[128,2048]{1,0:T(8,128)S(1)}) custom-call(bf16[272,2048]{1,0:T(8,128)(2,1)S(1)} %pad_maximum_fusion.e_ref, f32[272,2048]{1,0:T(8,128)} %get-tuple-element.30.q_ref, f32[144,2048]{1,0:T(8,128)S(1)} %copy-done.5, ...), custom_call_target="tpu_custom_call" | custom-call | flops 4000000000 | bytes 12000000 | tf_op jit(solution)/shard_map/pallas_call | solution.py:182
  108.6 4.2 %collective-permute-start.7 = (bf16[128,2048]{1,0:T(8,128)(2,1)S(1)}, bf16[128,2048]{1,0:T(8,128)(2,1)}, u32[]{:S(2)}, u32[]{:S(2)}) collective-permute-start(bf16[128,2048]{1,0:T(8,128)(2,1)S(1)} %get-tuple-element.34), channel_id=1, source_target_pairs={{1,16},{2,17},{3,18},{4,19},{5,20},{6,21},{7,22},{8,23},{9,24},{10... | collective-permute-start | bytes 1572872 | tf_op jit(solution)/shard_map/ppermute | solution.py:240
  112.8 0.3 collective-permute-start.6
  113.1 1.1 constant_dynamic-update-slice_fusion.6
  114.3 0.4 multiply_reduce_fusion
  114.7 0.8 copy-done.20
  115.4 0.1 copy.81.r_ref
  115.6 1.3 collective-permute-start.8
  116.9 14.3 %shard_map.113 = (f32[272,2048]{1,0:T(8,128)}, f32[144,2048]{1,0:T(8,128)S(1)}, f32[144,2048]{1,0:T(8,128)S(1)}, f32[144,2048]{1,0:T(8,128)S(1)}, bf16[256,2048]{1,0:T(8,128)(2,1)S(1)}, /*index=5*/f32[144,2048]{1,0:T(8,128)}) custom-call(bf16[416,2048]{1,0:T(8,128)(2,1)} %copy-done.20, f32[416,1]{1,0:T(8,128)S(1)} %copy.81.r_ref, f32[1,2048]{1,0:T(1,128)S(1)} %bitcast.75, ...), custom_call_target="tpu_custom_call" | custom-call | flops 4000000000 | bytes 12000000 | tf_op jit(solution)/shard_map/pallas_call | solution.py:166
  131.2 1.0 copy-done
  132.2 1.1 copy-done.2
  133.3 1.1 copy-done.11
  134.4 13.0 %shard_map.115 = (f32[1,2048]{1,0:T(1,128)S(1)}, f32[24,2048]{1,0:T(8,128)S(1)}, f32[128,256]{1,0:T(8,128)S(1)}) custom-call(bf16[128,2048]{1,0:T(8,128)(2,1)S(1)} %get-tuple-element.40.dg_ref, bf16[3,128,2048]{2,1,0:T(8,128)(2,1)} %get-tuple-element.41.da_ref, f32[128,2048]{1,0:T(8,128)S(1)} %copy-done.8, f32[144,2048]{1,0:T(8,128)S(1)} %copy-done.10, ...), custom_call_target="tpu_custom_call" | custom-call | flops 4000000000 | bytes 8000000 | tf_op jit(solution)/shard_map/pallas_call | solution.py:209
  147.5 0.1 copy.83.r_ref
  147.6 1.3 pad_maximum_fusion.1.e_ref
  148.9 1.3 copy-done.1
  150.2 1.3 copy-done.3
  151.4 15.3 %shard_map.114 = (bf16[128,2048]{1,0:T(8,128)(2,1)}, bf16[128,2048]{1,0:T(8,128)(2,1)S(1)}, bf16[3,128,2048]{2,1,0:T(8,128)(2,1)}, f32[128,2048]{1,0:T(8,128)S(1)}) custom-call(bf16[272,2048]{1,0:T(8,128)(2,1)S(1)} %pad_maximum_fusion.1.e_ref, f32[272,2048]{1,0:T(8,128)} %get-tuple-element.35.q_ref, f32[144,2048]{1,0:T(8,128)S(1)} %copy-done.1, ...), custom_call_target="tpu_custom_call" | custom-call | flops 4000000000 | bytes 12000000 | tf_op jit(solution)/shard_map/pallas_call | solution.py:182
  166.8 12.9 %shard_map.116 = (f32[1,2048]{1,0:T(1,128)S(1)}, f32[24,2048]{1,0:T(8,128)S(1)}, f32[128,256]{1,0:T(8,128)S(1)}) custom-call(bf16[128,2048]{1,0:T(8,128)(2,1)S(1)} %get-tuple-element.46.dg_ref, bf16[3,128,2048]{2,1,0:T(8,128)(2,1)} %get-tuple-element.47.da_ref, f32[128,2048]{1,0:T(8,128)S(1)} %get-tuple-element.48.du_ref, f32[144,2048]{1,0:T(8,128)S(1)} %copy-done.12, ...), custom_call_target="tpu_custom_call" | custom-call | flops 4000000000 | bytes 8000000 | tf_op jit(solution)/shard_map/pallas_call | solution.py:209
  180.2 0.2 copy.88
  180.4 0.2 copy.89
  180.7 0.8 copy.97
  181.5 0.6 dynamic-slice
  182.7 95.7 %all-reduce.10.cloned.1.call-done = f32[65536]{0:T(1024)} async-done(((f32[65536]{0:T(1024)}), f32[65536]{0:T(1024)}) %all-reduce.10.cloned.1.call-update) | async-done | bytes 262160
  278.4 0.7 dynamic-slice_multiply_fusion
  279.1 0.5 slice_bitcast_fusion.7
  279.6 0.6 reshape.147
  280.3 0.7 copy.90
  (124 shorter events, 2.5 us)
Async XLA Ops:
  7.2 20.0 %copy-start.25 = (f32[1,3,7,128]{3,0,2,1:T(1,128)S(1)}, f32[1,3,7,128]{3,0,2,1:T(1,128)}, u32[]{:S(2)}) copy-start(f32[1,3,7,128]{3,0,2,1:T(1,128)} %param.11) | copy-start | bytes 32260
  7.2 20.0 %copy-start.24 = (f32[3,7,128]{2,1,0:T(8,128)S(1)}, f32[3,7,128]{2,1,0:T(8,128)}, u32[]{:S(2)}) copy-start(f32[3,7,128]{2,1,0:T(8,128)} %param.14) | copy-start | bytes 32260
  7.2 20.0 %copy-start.26 = (f32[1,128,8]{1,2,0:T(8,128)S(1)}, f32[1,128,8]{1,2,0:T(8,128)}, u32[]{:S(2)}) copy-start(f32[1,128,8]{1,2,0:T(8,128)} %param.12) | copy-start | bytes 12292
  7.2 20.2 %copy-start.28 = (f32[1,128]{1,0:T(1,128)S(1)}, f32[1,128]{1,0:T(1,128)}, u32[]{:S(2)}) copy-start(f32[1,128]{1,0:T(1,128)} %param.10) | copy-start | bytes 1540
  7.2 20.3 %copy-start.27 = (f32[128,8]{0,1:T(8,128)S(1)}, f32[128,8]{0,1:T(8,128)}, u32[]{:S(2)}) copy-start(f32[128,8]{0,1:T(8,128)} %param.15) | copy-start | bytes 12292
  7.2 20.5 %copy-start.29 = (f32[128]{0:T(128)S(1)}, f32[128]{0:T(128)}, u32[]{:S(2)}) copy-start(f32[128]{0:T(128)} %param.13) | copy-start | bytes 1540
  7.2 20.5 %copy-start.23 = (bf16[1,128,2048]{2,1,0:T(8,128)(2,1)S(1)}, bf16[1,128,2048]{2,1,0:T(8,128)(2,1)}, u32[]{:S(2)}) copy-start(bf16[1,128,2048]{2,1,0:T(8,128)(2,1)} %param.9) | copy-start | bytes 1572868
  7.2 271.1 %all-reduce.10.cloned.1.call-start = ((), (), s32[]{:S(2)}) async-start(), calls=%async_computation | async-start | bytes 524288
  8.6 104.5 %collective-permute-start.11 = (bf16[128,2048]{1,0:T(8,128)(2,1)S(1)}, bf16[128,2048]{1,0:T(8,128)(2,1)}, u32[]{:S(2)}, u32[]{:S(2)}) collective-permute-start(bf16[128,2048]{1,0:T(8,128)(2,1)S(1)} %get-tuple-element.74.xf_ref.x_ref), channel_id=1, source_target_pairs={{1,0},{2,1},{3,2},{4,3},{5,4},{6,5},{7,6},{8,7},{9,8},{10,9},{11,1... | collective-permute-start | bytes 1572872 | tf_op jit(solution)/shard_map/ppermute | solution.py:230
  10.6 53.6 %collective-permute-start.10 = (bf16[128,2048]{1,0:T(8,128)(2,1)S(1)}, bf16[128,2048]{1,0:T(8,128)(2,1)}, u32[]{:S(2)}, u32[]{:S(2)}) collective-permute-start(bf16[128,2048]{1,0:T(8,128)(2,1)S(1)} %get-tuple-element.74.xf_ref.x_ref), channel_id=1, source_target_pairs={{0,1},{1,2},{2,3},{3,4},{4,5},{5,6},{6,7},{7,8},{8,9},{9,10},{10,1... | collective-permute-start | bytes 1572872 | tf_op jit(solution)/shard_map/ppermute | solution.py:230
  15.1 51.7 %collective-permute-start.4 = (bf16[128,2048]{1,0:T(8,128)(2,1)S(1)}, bf16[128,2048]{1,0:T(8,128)(2,1)}, u32[]{:S(2)}, u32[]{:S(2)}) collective-permute-start(bf16[128,2048]{1,0:T(8,128)(2,1)S(1)} %get-tuple-element.75.xf_ref.x_ref), channel_id=1, source_target_pairs={{1,0},{2,1},{3,2},{4,3},{5,4},{6,5},{7,6},{8,7},{9,8},{10,9},{11,1... | collective-permute-start | bytes 1572872 | tf_op jit(solution)/shard_map/ppermute | solution.py:230
  17.0 44.8 %collective-permute-start.3 = (bf16[128,2048]{1,0:T(8,128)(2,1)S(1)}, bf16[128,2048]{1,0:T(8,128)(2,1)}, u32[]{:S(2)}, u32[]{:S(2)}) collective-permute-start(bf16[128,2048]{1,0:T(8,128)(2,1)S(1)} %get-tuple-element.75.xf_ref.x_ref), channel_id=1, source_target_pairs={{0,1},{1,2},{2,3},{3,4},{4,5},{5,6},{6,7},{7,8},{8,9},{9,10},{10,1... | collective-permute-start | bytes 1572872 | tf_op jit(solution)/shard_map/ppermute | solution.py:230
  22.3 32.3 %collective-permute-start.2 = (bf16[16,2048]{1,0:T(8,128)(2,1)}, bf16[16,2048]{1,0:T(8,128)(2,1)S(1)}, u32[]{:S(2)}, u32[]{:S(2)}) collective-permute-start(bf16[16,2048]{1,0:T(8,128)(2,1)} %get-tuple-element.71), channel_id=1, source_target_pairs={{0,2},{1,3},{2,4},{3,5},{4,6},{5,7},{6,8},{7,9},{8,10},{9,11},{10,... | collective-permute-start | bytes 196616 | tf_op jit(solution)/shard_map/ppermute | solution.py:230
  52.1 1.1 copy-start.22
  53.3 0.9 slice-start
  54.3 12.3 %copy-start.17 = (bf16[2,1,128,2048]{3,2,1,0:T(8,128)(2,1)S(1)}, bf16[2,1,128,2048]{3,2,1,0:T(8,128)(2,1)}, u32[]{:S(2)}) copy-start(bf16[2,1,128,2048]{3,2,1,0:T(8,128)(2,1)} %param.8) | copy-start | bytes 3145732
  54.6 5.9 %collective-permute-start.9 = (bf16[16,2048]{1,0:T(8,128)(2,1)S(1)}, bf16[16,2048]{1,0:T(8,128)(2,1)S(1)}, u32[]{:S(2)}, u32[]{:S(2)}) collective-permute-start(bf16[16,2048]{1,0:T(8,128)(2,1)S(1)} %get-tuple-element.69), channel_id=1, source_target_pairs={{0,2},{1,3},{2,4},{3,5},{4,6},{5,7},{6,8},{7,9},{8,10},{9,11},{10,... | collective-permute-start | bytes 196616 | tf_op jit(solution)/shard_map/ppermute | solution.py:230
  60.6 31.2 %collective-permute-start.1 = (bf16[16,2048]{1,0:T(8,128)(2,1)S(1)}, bf16[16,2048]{1,0:T(8,128)(2,1)S(1)}, u32[]{:S(2)}, u32[]{:S(2)}) collective-permute-start(bf16[16,2048]{1,0:T(8,128)(2,1)S(1)} %slice_bitcast_fusion.6), channel_id=1, source_target_pairs={{2,0},{3,1},{4,2},{5,3},{6,4},{7,5},{8,6},{9,7},{10,8},{11,9},{12,... | collective-permute-start | bytes 196616 | tf_op jit(solution)/shard_map/ppermute | solution.py:230
  61.9 52.4 %collective-permute-start.12 = (bf16[16,2048]{1,0:T(8,128)(2,1)S(1)}, bf16[16,2048]{1,0:T(8,128)(2,1)S(1)}, u32[]{:S(2)}, u32[]{:S(2)}) collective-permute-start(bf16[16,2048]{1,0:T(8,128)(2,1)S(1)} %get-tuple-element.68), channel_id=1, source_target_pairs={{2,0},{3,1},{4,2},{5,3},{6,4},{7,5},{8,6},{9,7},{10,8},{11,9},{12,... | collective-permute-start | bytes 196616 | tf_op jit(solution)/shard_map/ppermute | solution.py:230
  64.3 7.7 %collective-permute-start.5 = (bf16[16,2048]{1,0:T(8,128)(2,1)S(1)}, bf16[16,2048]{1,0:T(8,128)(2,1)S(1)}, u32[]{:S(2)}, u32[]{:S(2)}) collective-permute-start(bf16[16,2048]{1,0:T(8,128)(2,1)S(1)} %get-tuple-element.70), channel_id=1, source_target_pairs={{2,0},{3,1},{4,2},{5,3},{6,4},{7,5},{8,6},{9,7},{10,8},{11,9},{12,... | collective-permute-start | bytes 196616 | tf_op jit(solution)/shard_map/ppermute | solution.py:230
  66.8 1.2 copy-start.18
  68.0 23.9 %collective-permute-start = (bf16[128,2048]{1,0:T(8,128)(2,1)S(1)}, bf16[128,2048]{1,0:T(8,128)(2,1)}, u32[]{:S(2)}, u32[]{:S(2)}) collective-permute-start(bf16[128,2048]{1,0:T(8,128)(2,1)S(1)} %bitcast.96), channel_id=1, source_target_pairs={{1,0},{2,1},{3,2},{4,3},{5,4},{6,5},{7,6},{8,7},{9,8},{10,9},{11,1... | collective-permute-start | bytes 1572872 | tf_op jit(solution)/shard_map/ppermute | solution.py:230
  72.0 1.2 copy-start.21
  87.4 1.1 copy-start.4
  88.5 1.1 copy-start.6
  89.6 1.0 copy-start.9
  90.6 1.0 copy-start.13
  91.8 1.4 copy-start.5
  93.2 19.9 %copy-start.19 = (bf16[416,2048]{1,0:T(8,128)(2,1)S(1)}, bf16[416,2048]{1,0:T(8,128)(2,1)}, u32[]{:S(2)}) copy-start(bf16[416,2048]{1,0:T(8,128)(2,1)} %copy-done.18) | copy-start | bytes 5111812
  108.6 6.0 %copy-start.7 = (f32[128,2048]{1,0:T(8,128)}, f32[128,2048]{1,0:T(8,128)S(1)}, u32[]{:S(2)}) copy-start(f32[128,2048]{1,0:T(8,128)S(1)} %get-tuple-element.42.du_ref) | copy-start | bytes 3145732
  108.6 39.0 %collective-permute-start.7 = (bf16[128,2048]{1,0:T(8,128)(2,1)S(1)}, bf16[128,2048]{1,0:T(8,128)(2,1)}, u32[]{:S(2)}, u32[]{:S(2)}) collective-permute-start(bf16[128,2048]{1,0:T(8,128)(2,1)S(1)} %get-tuple-element.34), channel_id=1, source_target_pairs={{1,16},{2,17},{3,18},{4,19},{5,20},{6,21},{7,22},{8,23},{9,24},{10... | collective-permute-start | bytes 1572872 | tf_op jit(solution)/shard_map/ppermute | solution.py:240
  112.8 34.8 %collective-permute-start.6 = (bf16[128,2048]{1,0:T(8,128)(2,1)S(1)}, bf16[128,2048]{1,0:T(8,128)(2,1)}, u32[]{:S(2)}, u32[]{:S(2)}) collective-permute-start(bf16[128,2048]{1,0:T(8,128)(2,1)S(1)} %get-tuple-element.34), channel_id=1, source_target_pairs={{0,16},{1,17},{2,18},{3,19},{4,20},{5,21},{6,22},{7,23},{8,24},{9,... | collective-permute-start | bytes 1572872 | tf_op jit(solution)/shard_map/ppermute | solution.py:240
  114.2 1.2 copy-start.20
  115.6 32.0 %collective-permute-start.8 = (bf16[16,2048]{1,0:T(8,128)(2,1)S(1)}, bf16[16,2048]{1,0:T(8,128)(2,1)S(1)}, u32[]{:S(2)}, u32[]{:S(2)}) collective-permute-start(bf16[16,2048]{1,0:T(8,128)(2,1)S(1)} %slice.109), channel_id=1, source_target_pairs={{2,16},{3,17},{4,18},{5,19},{6,20},{7,21},{8,22},{9,23},{10,24},{1... | collective-permute-start | bytes 196616 | tf_op jit(solution)/shard_map/ppermute | solution.py:240
  116.9 17.5 %copy-start.8 = (f32[128,2048]{1,0:T(8,128)S(1)}, f32[128,2048]{1,0:T(8,128)}, u32[]{:S(2)}) copy-start(f32[128,2048]{1,0:T(8,128)} %copy-done.7) | copy-start | bytes 3145732
  116.9 17.5 %copy-start.10 = (f32[144,2048]{1,0:T(8,128)S(1)}, f32[144,2048]{1,0:T(8,128)}, u32[]{:S(2)}) copy-start(f32[144,2048]{1,0:T(8,128)} %copy-done.9) | copy-start | bytes 3538948
  116.9 17.5 %copy-start.14 = (bf16[256,2048]{1,0:T(8,128)(2,1)S(1)}, bf16[256,2048]{1,0:T(8,128)(2,1)}, u32[]{:S(2)}) copy-start(bf16[256,2048]{1,0:T(8,128)(2,1)} %copy-done.13) | copy-start | bytes 3145732
  131.2 1.0 copy-start
  132.2 1.1 copy-start.2
  133.3 1.1 copy-start.11
  134.4 13.0 %copy-start.15 = (bf16[256,2048]{1,0:T(8,128)(2,1)}, bf16[256,2048]{1,0:T(8,128)(2,1)S(1)}, u32[]{:S(2)}) copy-start(bf16[256,2048]{1,0:T(8,128)(2,1)S(1)} %get-tuple-element.50.w_ref) | copy-start | bytes 3145732
  148.9 1.3 copy-start.1
  150.2 1.3 copy-start.3
  151.4 15.3 %copy-start.12 = (f32[144,2048]{1,0:T(8,128)S(1)}, f32[144,2048]{1,0:T(8,128)}, u32[]{:S(2)}) copy-start(f32[144,2048]{1,0:T(8,128)} %copy-done.11) | copy-start | bytes 3538948
  151.4 15.3 %copy-start.16 = (bf16[256,2048]{1,0:T(8,128)(2,1)S(1)}, bf16[256,2048]{1,0:T(8,128)(2,1)}, u32[]{:S(2)}) copy-start(bf16[256,2048]{1,0:T(8,128)(2,1)} %copy-done.15) | copy-start | bytes 3145732
  180.1 1.4 copy-start.30
Sparse Core Ops, SparseCore 0:
  181.6 96.7 all-reduce.9

commit v2 on v1

--- a/solution.py
+++ b/solution.py
@@ -224,6 +224,152 @@
     )(dg, da, du, u, w, x, r)
 
 
+def greet(me, count):
+    barrier = pltpu.get_barrier_semaphore()
+
+    def signal(d, carry):
+        pl.semaphore_signal(barrier, inc=1, device_id={"fsdp": lax.rem(me + d, count)})
+        return carry
+
+    lax.fori_loop(1, count, signal, 0)
+    pl.semaphore_wait(barrier, count - 1)
+
+
+def start_kernel(
+    count, flat_ref, x_ref, e_ref, every_ref, xe_ref, ee_ref, send, recv, halo_send, halo_recv
+):
+    me = lax.axis_index("fsdp")
+    rows = x_ref.shape[0]
+    halos = (
+        (x_ref, 0, rows, xe_ref, EDGE, 1),
+        (e_ref, 0, rows, ee_ref, rows, -1),
+        (x_ref, 0, rows, xe_ref, EDGE + 2 * rows, -1),
+        (x_ref, rows - EDGE, EDGE, xe_ref, 0, 2),
+        (x_ref, 0, EDGE, xe_ref, EDGE + 3 * rows, -2),
+        (e_ref, 0, EDGE, ee_ref, 2 * rows, -2),
+    )
+
+    def halo(i, target):
+        source, first, size, landing, place, _ = halos[i]
+        return pltpu.make_async_remote_copy(
+            src_ref=source.at[pl.ds(first, size)],
+            dst_ref=landing.at[pl.ds(place, size)],
+            send_sem=halo_send.at[i],
+            recv_sem=halo_recv.at[i],
+            device_id={"fsdp": target},
+        )
+
+    def share(d):
+        return pltpu.make_async_remote_copy(
+            src_ref=flat_ref,
+            dst_ref=every_ref.at[me],
+            send_sem=send.at[d],
+            recv_sem=recv.at[d],
+            device_id={"fsdp": lax.rem(me + d, count)},
+        )
+
+    def sends(steps):
+        return (me + steps >= 0) & (me + steps < count)
+
+    greet(me, count)
+
+    def begin(d, carry):
+        share(d).start()
+        return carry
+
+    lax.fori_loop(1, count, begin, 0)
+    for i, item in enumerate(halos):
+
+        @pl.when(sends(item[5]))
+        def _(i=i, steps=item[5]):
+            halo(i, me + steps).start()
+
+    every_ref[me] = flat_ref[...]
+    xe_ref[EDGE + rows : EDGE + 2 * rows] = x_ref[...]
+    ee_ref[:rows] = e_ref[...]
+    for i, (_, _, size, landing, place, steps) in enumerate(halos):
+
+        @pl.when(sends(-steps))
+        def _(i=i, steps=steps):
+            halo(i, me - steps).wait_recv()
+
+        @pl.when(jnp.logical_not(sends(-steps)))
+        def _(size=size, landing=landing, place=place):
+            landing[place : place + size] = jnp.zeros((size, landing.shape[1]), landing.dtype)
+
+        @pl.when(sends(steps))
+        def _(i=i, steps=steps):
+            halo(i, me + steps).wait_send()
+
+    def finish(d, carry):
+        share(d).wait()
+        return carry
+
+    lax.fori_loop(1, count, finish, 0)
+
+
+def scatter_kernel(count, packed_ref, out_ref, landed, send, recv):
+    me = lax.axis_index("fsdp")
+
+    def share(d):
+        peer = lax.rem(me + d, count)
+        return pltpu.make_async_remote_copy(
+            src_ref=packed_ref.at[peer],
+            dst_ref=landed.at[d],
+            send_sem=send.at[d],
+            recv_sem=recv.at[d],
+            device_id={"fsdp": peer},
+        )
+
+    greet(me, count)
+
+    def begin(d, carry):
+        share(d).start()
+        return carry
+
+    lax.fori_loop(1, count, begin, 0)
+    out_ref[...] = packed_ref[me]
+
+    def finish(d, carry):
+        share(d).wait()
+        out_ref[...] += landed[d]
+        return carry
+
+    lax.fori_loop(1, count, finish, 0)
+
+
+def run_start(flat, x, e, shards):
+    rows, channels = x.shape
+    vmem = pl.BlockSpec(memory_space=pltpu.VMEM)
+    dma = pltpu.SemaphoreType.DMA
+    return pl.pallas_call(
+        lambda *refs: start_kernel(shards, *refs),
+        in_specs=[vmem] * 3,
+        out_specs=[vmem] * 3,
+        out_shape=[
+            jax.ShapeDtypeStruct((shards,) + flat.shape, F32),
+            jax.ShapeDtypeStruct((3 * rows + 2 * EDGE, channels), BF16),
+            jax.ShapeDtypeStruct((2 * rows + EDGE, channels), BF16),
+        ],
+        scratch_shapes=[dma((shards,)), dma((shards,)), dma((6,)), dma((6,))],
+        compiler_params=pltpu.CompilerParams(collective_id=0, has_side_effects=True, **PARAMS),
+    )(flat, x, e)
+
+
+def run_scatter(packed):
+    shards = packed.shape[0]
+    vmem = pl.BlockSpec(memory_space=pltpu.VMEM)
+    dma = pltpu.SemaphoreType.DMA
+    return pl.pallas_call(
+        lambda *refs: scatter_kernel(shards, *refs),
+        in_specs=[vmem],
+        out_specs=vmem,
+        out_shape=jax.ShapeDtypeStruct(packed.shape[1:], F32),
+        scratch_shapes=[pltpu.VMEM(packed.shape, F32), dma((shards,)), dma((shards,))],
+        compiler_params=pltpu.CompilerParams(collective_id=1, has_side_effects=True, **PARAMS),
+    )(packed)
+
+
 def shifted(value, steps):
     count = lax.axis_size("fsdp")
     initial, last = (max(0, -steps), min(count, count - steps))
@@ -253,7 +399,12 @@
             jnp.concatenate([lower_gain, lower_short.reshape(-1), lower_medium.reshape(-1)]),
         ]
     )
-    every = lax.all_gather(flat, "fsdp", axis=0, tiled=False)
+    x1, x2, e1 = inputs[0, 0], inputs[1, 0], top_grad[0]
+    extent = flat.shape[1]
+    room = -(-extent // 1024) * 1024
+    flat = jnp.pad(flat, ((0, 0), (0, room - extent))).reshape(-1, LANES)
+    every, x1_ext, e1_ext = run_start(flat, x1, e1, shards)
+    every = every.reshape(shards, 2, room)[:, :, :extent]
 
     def layer_params(part):
         gain = part[:, :chunk].reshape(1, channels)
@@ -274,23 +425,22 @@
 
     def extended(x):
         rows = x.shape[0]
-        x_ext = jnp.concatenate(
+        return jnp.concatenate(
             [
                 shifted(x[rows - EDGE :], 2), shifted(x, 1), x, shifted(x, -1),
                 shifted(x[:EDGE], -2),
             ]
         )
+
+    def row_scale(x_ext):
         wide = x_ext.astype(F32)
-        r_ext = lax.rsqrt(jnp.mean(wide * wide, axis=-1, keepdims=True) + NORM_EPS)
-        return x_ext, r_ext
+        return lax.rsqrt(jnp.mean(wide * wide, axis=-1, keepdims=True) + NORM_EPS)
 
     def terms_of(x, r, ahead, back):
         return run_terms(back[1], back[2], back[3], ahead[3], ahead[4], x, r)
 
-    x1, x2, e1 = inputs[0, 0], inputs[1, 0], top_grad[0]
-    e1_ext = jnp.concatenate([e1, shifted(e1, -1), shifted(e1[:EDGE], -2)])
-    x1_ext, r1_ext = extended(x1)
-    x2_ext, r2_ext = extended(x2)
+    x2_ext = extended(x2)
+    r1_ext, r2_ext = row_scale(x1_ext), row_scale(x2_ext)
     own_rows = slice(TAPS + EDGE, 2 * TAPS + EDGE)
     r1, r2 = r1_ext[own_rows], r2_ext[own_rows]
     (gain1, short1, causal1, anti1), (gain2, short2, causal2, anti2) = params
@@ -318,8 +468,8 @@
     factor = (x1.shape[0] * shards) ** (-0.5)
     width = packed.shape[1]
     room = -(-width // 1024) * 1024
-    packed = jnp.pad(packed, ((0, 0), (0, room - width))).reshape(shards * room)
-    summed = lax.psum_scatter(packed, "fsdp", scatter_dimension=0, tiled=True) * factor
+    packed = jnp.pad(packed, ((0, 0), (0, room - width))).reshape(shards, -1, LANES)
+    summed = run_scatter(packed).reshape(-1) * factor
     return (
         back2[0][None],
         summed[:chunk][None],

time: 291 us -> 188 us (0.65)
  waiting for transfers between devices: 97 us -> 4.04 us
  Pallas kernels: 85 us -> 131 us
  blocking collectives: 23.9 us -> 0 us
  starting transfers between devices: 34.1 us -> 16.1 us
  between operations: 15.6 us -> 1.36 us
    unnamed x2 -> x0, waiting for transfers between devices: 95.7 us -> none
    pallas_call x0 -> x2, Pallas kernels: none -> 45.4 us  [the longest x1 33.4 us: run_start(): pl.pallas_call(lambda *refs: start_kernel(shards, *refs), in_specs=[vmem]...]
    all_gather x1 -> x0, blocking collectives: 23.9 us -> none  [on_device(): every = lax.all_gather(flat, 'fsdp', axis=0, tiled=False)]
    ppermute x10 -> x4, starting transfers between devices: 28.3 us -> 11.5 us  [shifted(): lax.ppermute(value, 'fsdp', [(source, source + steps) for source in range...]
    unnamed x81 -> x70, local copies, waits for them, and re-layouts: 19.8 us -> 12.4 us
  transfers between devices with their start and end apart: 14 -> 7, of which waited for: 2 -> 1; matrix products, arithmetic and copies ran while one was open for 4% -> 4% of each run, Pallas kernels for 20% -> 15%
where the time goes in v2:
time: 188 us; the launch traced here: 185 us
  Pallas kernels  131 us (70%)
  local copies, waits for them, and re-layouts  27.9 us (15%)
  starting transfers between devices  16.1 us (9%)
  other arithmetic  5.06 us (3%)
  waiting for transfers between devices  4.04 us (2%)
    pallas_call x1, Pallas kernels, run_start(): pl.pallas_call(lambda *refs: start_kernel(shards, *refs), in_specs=[vmem]...  33.4 us
    pallas_call x2, Pallas kernels, run_backward(): pl.pallas_call(backward_kernel, grid=(blocks,), in_specs=[tall(TAPS + own...  31.1 us
    pallas_call x2, Pallas kernels, run_forward(): pl.pallas_call(forward_kernel, grid=(channels // LANES,), in_specs=[tall(...  28.3 us
    pallas_call x2, Pallas kernels, run_terms(): pl.pallas_call(terms_kernel, grid=(channels // LANES,), in_specs=[tall(TA...  25.9 us
    unnamed x70, local copies, waits for them, and re-layouts  12.4 us
    pallas_call x1, Pallas kernels, run_scatter(): pl.pallas_call(lambda *refs: scatter_kernel(shards, *refs), in_specs=[vme...  11.9 us
    ppermute x4, starting transfers between devices, shifted(): lax.ppermute(value, 'fsdp', [(source, source + steps) for source in range...  11.5 us
    ppermute x3, starting transfers between devices, crossed(): return lax.ppermute(value, ('section', 'fsdp'), pairs)  4.54 us
  transfers between devices with their start and end apart: 7, of which 1 were waited for; matrix products, arithmetic and copies ran while one was open for 4% of the time, Pallas kernels for 15%

profile of v2, /device:TPU:1, one launch (start us, length us, event | category | flops | bytes accessed | tf_op | source)
XLA Modules:
  0.0 185.1 jit_solution(14491749325305615394)
XLA Ops:
  0.7 2.1 %slice_bitcast_fusion.2 = (bf16[128,2048]{1,0:T(8,128)(2,1)}, bf16[128,2048]{1,0:T(8,128)(2,1)S(1)}) fusion(bf16[2,1,128,2048]{3,2,1,0:T(8,128)(2,1)} %param.8), kind=kLoop, calls=%fused_computation.10 | loop fusion | bytes 2097152 | tf_op jit(solution)/shard_map/squeeze | solution.py:402
  2.8 0.1 copy.24
  2.9 0.1 reshape.144
  3.2 0.1 copy.25
  3.3 0.1 reshape.146
  3.5 33.4 %shard_map.111 = (f32[16,64,128]{2,1,0:T(8,128)S(1)}, bf16[416,2048]{1,0:T(8,128)(2,1)S(1)}, bf16[272,2048]{1,0:T(8,128)(2,1)S(1)}) custom-call(f32[64,128]{1,0:T(8,128)S(1)} %reshape.147.refs_0_, bf16[128,2048]{1,0:T(8,128)(2,1)S(1)} %get-tuple-element.73.refs_1_.xf_ref.x_ref, bf16[128,2048]{1,0:T(8,128)(2,1)S(1)} %bitcast.77), custom_call_target="tpu_custom_call" | custom-call | tf_op jit(solution)/shard_map/pallas_call | solution.py:345
  37.0 1.0 copy-done.3
  37.9 2.6 %copy.52 = f32[16,64,128]{0,2,1:T(8,128)} copy(f32[16,64,128]{2,1,0:T(8,128)S(1)} %get-tuple-element.35) | data formatting | bytes 1048576 | tf_op jit(solution)/shard_map/reshape | solution.py:407
  40.6 1.7 slice_bitcast_fusion.1
  42.3 1.3 slice.108
  43.6 0.5 copy-done.19
  44.1 1.8 copy.29
  45.8 0.2 copy.30
  46.1 0.1 copy.31
  46.4 0.1 pad.31.table_ref
  46.6 0.4 multiply_reduce_fusion.1
  47.1 0.1 copy.32.r_ref
  47.2 0.1 copy.34.r_ref
  47.4 14.2 %shard_map.112 = (f32[272,2048]{1,0:T(8,128)}, f32[144,2048]{1,0:T(8,128)S(1)}, f32[144,2048]{1,0:T(8,128)S(1)}, f32[144,2048]{1,0:T(8,128)S(1)}, bf16[256,2048]{1,0:T(8,128)(2,1)S(1)}, /*index=5*/f32[144,2048]{1,0:T(8,128)}) custom-call(bf16[416,2048]{1,0:T(8,128)(2,1)} %copy-done, f32[416,1]{1,0:T(8,128)S(1)} %copy.32.r_ref, f32[1,2048]{1,0:T(1,128)S(1)} %bitcast.80, ...), custom_call_target="tpu_custom_call" | custom-call | flops 4000000000 | bytes 12000000 | tf_op jit(solution)/shard_map/pallas_call | solution.py:166
  61.5 1.0 copy-done.7
  62.6 1.0 copy-done.14
  63.6 15.8 %shard_map.113 = (bf16[128,2048]{1,0:T(8,128)(2,1)S(1)}, bf16[128,2048]{1,0:T(8,128)(2,1)S(1)}, bf16[3,128,2048]{2,1,0:T(8,128)(2,1)}, f32[128,2048]{1,0:T(8,128)S(1)}) custom-call(bf16[272,2048]{1,0:T(8,128)(2,1)S(1)} %copy-done.4, f32[272,2048]{1,0:T(8,128)} %get-tuple-element.36.q_ref, f32[144,2048]{1,0:T(8,128)S(1)} %get-tuple-element.37.k_ref, ...), custom_call_target="tpu_custom_call" | custom-call | flops 4000000000 | bytes 12000000 | tf_op jit(solution)/shard_map/pallas_call | solution.py:182
  79.3 1.0 copy-done.8
  80.3 1.2 collective-permute-start
  81.5 1.9 %collective-permute-start.1 = (bf16[128,2048]{1,0:T(8,128)(2,1)S(1)}, bf16[128,2048]{1,0:T(8,128)(2,1)}, u32[]{:S(2)}, u32[]{:S(2)}) collective-permute-start(bf16[128,2048]{1,0:T(8,128)(2,1)S(1)} %get-tuple-element.40), channel_id=1, source_target_pairs={{1,16},{2,17},{3,18},{4,19},{5,20},{6,21},{7,22},{8,23},{9,24},{10... | collective-permute-start | bytes 1572872 | tf_op jit(solution)/shard_map/ppermute | solution.py:386
  83.4 4.0 %collective-permute-start.4 = (bf16[128,2048]{1,0:T(8,128)(2,1)S(1)}, bf16[128,2048]{1,0:T(8,128)(2,1)}, u32[]{:S(2)}, u32[]{:S(2)}) collective-permute-start(bf16[128,2048]{1,0:T(8,128)(2,1)S(1)} %copy-done.2), channel_id=1, source_target_pairs={{0,1},{1,2},{2,3},{3,4},{4,5},{5,6},{6,7},{7,8},{8,9},{9,10},{10,1... | collective-permute-start | bytes 1572872 | tf_op jit(solution)/shard_map/ppermute | solution.py:376
  87.4 1.9 %collective-permute-start.5 = (bf16[128,2048]{1,0:T(8,128)(2,1)S(1)}, bf16[128,2048]{1,0:T(8,128)(2,1)}, u32[]{:S(2)}, u32[]{:S(2)}) collective-permute-start(bf16[128,2048]{1,0:T(8,128)(2,1)S(1)} %copy-done.2), channel_id=1, source_target_pairs={{1,0},{2,1},{3,2},{4,3},{5,4},{6,5},{7,6},{8,7},{9,8},{10,9},{11,1... | collective-permute-start | bytes 1572872 | tf_op jit(solution)/shard_map/ppermute | solution.py:376
  89.4 1.5 slice_bitcast_fusion.4
  90.9 4.3 %collective-permute-start.3 = (bf16[16,2048]{1,0:T(8,128)(2,1)}, bf16[16,2048]{1,0:T(8,128)(2,1)S(1)}, u32[]{:S(2)}, u32[]{:S(2)}) collective-permute-start(bf16[16,2048]{1,0:T(8,128)(2,1)} %get-tuple-element.71), channel_id=1, source_target_pairs={{0,2},{1,3},{2,4},{3,5},{4,6},{5,7},{6,8},{7,9},{8,10},{9,11},{10,... | collective-permute-start | bytes 196616 | tf_op jit(solution)/shard_map/ppermute | solution.py:376
  95.3 2.5 %fusion = f32[16,3840]{0,1:T(8,128)S(1)} fusion(f32[16,2,4096]{0,2,1:T(8,128)} %bitcast.83, pred[]{:T(512)S(6)} %eq.3), kind=kLoop, calls=%fused_computation.3 | loop fusion | flops 61440 | bytes 737281 | tf_op jit(solution)/shard_map/jit(_where)/select_n | solution.py:424
  97.8 0.2 copy-done.11
  98.0 0.3 copy-done.15
  98.3 13.0 %shard_map.116 = (f32[1,2048]{1,0:T(1,128)S(1)}, f32[24,2048]{1,0:T(8,128)S(1)}, f32[128,256]{1,0:T(8,128)S(1)}) custom-call(bf16[128,2048]{1,0:T(8,128)(2,1)S(1)} %get-tuple-element.46.dg_ref, bf16[3,128,2048]{2,1,0:T(8,128)(2,1)} %get-tuple-element.47.da_ref, f32[128,2048]{1,0:T(8,128)S(1)} %copy-done.9, f32[144,2048]{1,0:T(8,128)S(1)} %copy-done.11, ...), custom_call_target="tpu_custom_call" | custom-call | flops 4000000000 | bytes 8000000 | tf_op jit(solution)/shard_map/pallas_call | solution.py:209
  111.4 0.1 slice.112
  111.5 0.2 copy.39
  111.7 0.1 copy.40
  111.9 0.4 copy.38
  112.4 0.1 pad.34.table_ref
  112.6 1.4 collective-permute-start.2
  114.0 1.3 collective-permute-start.6
  115.3 1.1 constant_dynamic-update-slice_fusion.3
  116.5 1.1 constant_dynamic-update-slice_fusion.1
  117.6 4.0 %collective-permute-done.6 = bf16[16,2048]{1,0:T(8,128)(2,1)S(1)} collective-permute-done((bf16[16,2048]{1,0:T(8,128)(2,1)}, bf16[16,2048]{1,0:T(8,128)(2,1)S(1)}, u32[]{:S(2)}, u32[]{:S(2)}) %collective-permute-start.6) | collective-permute-done | bytes 65568 | tf_op jit(solution)/shard_map/ppermute | solution.py:376
  121.6 0.4 multiply_reduce_fusion
  122.0 0.8 copy-done.21
  122.8 0.1 copy.41.r_ref
  123.0 14.1 %shard_map.114 = (f32[272,2048]{1,0:T(8,128)}, f32[144,2048]{1,0:T(8,128)S(1)}, f32[144,2048]{1,0:T(8,128)S(1)}, f32[144,2048]{1,0:T(8,128)S(1)}, bf16[256,2048]{1,0:T(8,128)(2,1)S(1)}, /*index=5*/f32[144,2048]{1,0:T(8,128)}) custom-call(bf16[416,2048]{1,0:T(8,128)(2,1)} %copy-done.21, f32[416,1]{1,0:T(8,128)S(1)} %copy.41.r_ref, f32[1,2048]{1,0:T(1,128)S(1)} %bitcast.78, ...), custom_call_target="tpu_custom_call" | custom-call | flops 4000000000 | bytes 12000000 | tf_op jit(solution)/shard_map/pallas_call | solution.py:166
  137.1 1.1 copy-done.5
  138.1 1.0 copy-done.12
  139.2 1.0 copy-done.16
  140.2 0.1 copy.43.r_ref
  140.4 1.4 pad_maximum_fusion.e_ref
  141.8 0.1 copy-done.6
  141.9 15.3 %shard_map.115 = (bf16[128,2048]{1,0:T(8,128)(2,1)}, bf16[128,2048]{1,0:T(8,128)(2,1)S(1)}, bf16[3,128,2048]{2,1,0:T(8,128)(2,1)}, f32[128,2048]{1,0:T(8,128)S(1)}) custom-call(bf16[272,2048]{1,0:T(8,128)(2,1)S(1)} %pad_maximum_fusion.e_ref, f32[272,2048]{1,0:T(8,128)} %get-tuple-element.41.q_ref, f32[144,2048]{1,0:T(8,128)S(1)} %get-tuple-element.42.k_ref, ...), custom_call_target="tpu_custom_call" | custom-call | flops 4000000000 | bytes 12000000 | tf_op jit(solution)/shard_map/pallas_call | solution.py:182
  157.3 12.9 %shard_map.117 = (f32[1,2048]{1,0:T(1,128)S(1)}, f32[24,2048]{1,0:T(8,128)S(1)}, f32[128,256]{1,0:T(8,128)S(1)}) custom-call(bf16[128,2048]{1,0:T(8,128)(2,1)S(1)} %get-tuple-element.52.dg_ref, bf16[3,128,2048]{2,1,0:T(8,128)(2,1)} %get-tuple-element.53.da_ref, f32[128,2048]{1,0:T(8,128)S(1)} %get-tuple-element.54.du_ref, f32[144,2048]{1,0:T(8,128)S(1)} %copy-done.13, ...), custom_call_target="tpu_custom_call" | custom-call | flops 4000000000 | bytes 8000000 | tf_op jit(solution)/shard_map/pallas_call | solution.py:209
  170.4 0.1 slice_add_fusion.1
  170.5 0.1 copy.47
  170.7 0.3 copy.48
  170.9 0.2 copy.49
  171.2 11.9 %shard_map.118 = f32[32,128]{1,0:T(8,128)S(1)} custom-call(f32[16,32,128]{2,1,0:T(8,128)S(1)} %bitcast.76), custom_call_target="tpu_custom_call" | custom-call | tf_op jit(solution)/shard_map/pallas_call | solution.py:363
  183.2 0.5 slice.118
  183.7 0.1 reshape.162
  183.8 0.7 copy.51
  184.4 0.6 reshape.167
  (97 shorter events, 1.4 us)
Async XLA Ops:
  0.6 2.2 %copy-start.24 = (f32[1,128,8]{1,2,0:T(8,128)S(1)}, f32[1,128,8]{1,2,0:T(8,128)}, u32[]{:S(2)}) copy-start(f32[1,128,8]{1,2,0:T(8,128)} %param.12) | copy-start | bytes 12292
  0.6 2.4 %copy-start.23 = (f32[1,3,7,128]{3,0,2,1:T(1,128)S(1)}, f32[1,3,7,128]{3,0,2,1:T(1,128)}, u32[]{:S(2)}) copy-start(f32[1,3,7,128]{3,0,2,1:T(1,128)} %param.11) | copy-start | bytes 32260
  0.7 2.4 %copy-start.26 = (f32[1,128]{1,0:T(1,128)S(1)}, f32[1,128]{1,0:T(1,128)}, u32[]{:S(2)}) copy-start(f32[1,128]{1,0:T(1,128)} %param.10) | copy-start | bytes 1540
  0.7 2.5 %copy-start.25 = (f32[128,8]{0,1:T(8,128)S(1)}, f32[128,8]{0,1:T(8,128)}, u32[]{:S(2)}) copy-start(f32[128,8]{0,1:T(8,128)} %param.15) | copy-start | bytes 12292
  0.7 2.7 %copy-start.22 = (f32[3,7,128]{2,1,0:T(8,128)S(1)}, f32[3,7,128]{2,1,0:T(8,128)}, u32[]{:S(2)}) copy-start(f32[3,7,128]{2,1,0:T(8,128)} %param.14) | copy-start | bytes 32260
  0.7 2.7 %copy-start.27 = (f32[128]{0:T(128)S(1)}, f32[128]{0:T(128)}, u32[]{:S(2)}) copy-start(f32[128]{0:T(128)} %param.13) | copy-start | bytes 1540
  0.7 2.8 %copy-start.1 = (bf16[1,128,2048]{2,1,0:T(8,128)(2,1)S(1)}, bf16[1,128,2048]{2,1,0:T(8,128)(2,1)}, u32[]{:S(2)}) copy-start(bf16[1,128,2048]{2,1,0:T(8,128)(2,1)} %param.9) | copy-start | bytes 1572868
  36.9 1.0 copy-start.3
  37.9 8.6 %copy-start = (bf16[416,2048]{1,0:T(8,128)(2,1)}, bf16[416,2048]{1,0:T(8,128)(2,1)S(1)}, u32[]{:S(2)}) copy-start(bf16[416,2048]{1,0:T(8,128)(2,1)S(1)} %get-tuple-element.34.x_ref) | copy-start | bytes 5111812
  42.3 1.8 copy-start.19
  44.1 2.4 %slice-start.1 = ((f32[16,3840]{0,1:T(8,128)}), f32[16,128]{0,1:T(8,128)S(1)}, s32[]{:S(2)}) async-start(f32[16,3840]{0,1:T(8,128)} %copy-done.19), calls=%async_computation.1 | async-start | bytes 131072 | tf_op jit(solution)/shard_map/slice | solution.py:410
  47.3 16.2 %copy-start.4 = (bf16[272,2048]{1,0:T(8,128)(2,1)S(1)}, bf16[272,2048]{1,0:T(8,128)(2,1)}, u32[]{:S(2)}) copy-start(bf16[272,2048]{1,0:T(8,128)(2,1)} %copy-done.3) | copy-start | bytes 3342340
  61.5 1.0 copy-start.7
  62.6 1.0 copy-start.14
  63.6 15.8 %copy-start.10 = (f32[144,2048]{1,0:T(8,128)}, f32[144,2048]{1,0:T(8,128)S(1)}, u32[]{:S(2)}) copy-start(f32[144,2048]{1,0:T(8,128)S(1)} %get-tuple-element.49.u_ref) | copy-start | bytes 3538948
  63.6 19.9 %copy-start.2 = (bf16[128,2048]{1,0:T(8,128)(2,1)S(1)}, bf16[128,2048]{1,0:T(8,128)(2,1)}, u32[]{:S(2)}) copy-start(bf16[128,2048]{1,0:T(8,128)(2,1)} %get-tuple-element.72.xf_ref.x_ref) | copy-start | bytes 1572868
  79.3 1.0 copy-start.8
  80.3 60.0 %collective-permute-start = (bf16[128,2048]{1,0:T(8,128)(2,1)S(1)}, bf16[128,2048]{1,0:T(8,128)(2,1)}, u32[]{:S(2)}, u32[]{:S(2)}) collective-permute-start(bf16[128,2048]{1,0:T(8,128)(2,1)S(1)} %get-tuple-element.40), channel_id=1, source_target_pairs={{0,16},{1,17},{2,18},{3,19},{4,20},{5,21},{6,22},{7,23},{8,24},{9,... | collective-permute-start | bytes 1572872 | tf_op jit(solution)/shard_map/ppermute | solution.py:386
  81.5 58.8 %collective-permute-start.1 = (bf16[128,2048]{1,0:T(8,128)(2,1)S(1)}, bf16[128,2048]{1,0:T(8,128)(2,1)}, u32[]{:S(2)}, u32[]{:S(2)}) collective-permute-start(bf16[128,2048]{1,0:T(8,128)(2,1)S(1)} %get-tuple-element.40), channel_id=1, source_target_pairs={{1,16},{2,17},{3,18},{4,19},{5,20},{6,21},{7,22},{8,23},{9,24},{10... | collective-permute-start | bytes 1572872 | tf_op jit(solution)/shard_map/ppermute | solution.py:386
  83.4 30.6 %collective-permute-start.4 = (bf16[128,2048]{1,0:T(8,128)(2,1)S(1)}, bf16[128,2048]{1,0:T(8,128)(2,1)}, u32[]{:S(2)}, u32[]{:S(2)}) collective-permute-start(bf16[128,2048]{1,0:T(8,128)(2,1)S(1)} %copy-done.2), channel_id=1, source_target_pairs={{0,1},{1,2},{2,3},{3,4},{4,5},{5,6},{6,7},{7,8},{8,9},{9,10},{10,1... | collective-permute-start | bytes 1572872 | tf_op jit(solution)/shard_map/ppermute | solution.py:376
  87.4 29.1 %collective-permute-start.5 = (bf16[128,2048]{1,0:T(8,128)(2,1)S(1)}, bf16[128,2048]{1,0:T(8,128)(2,1)}, u32[]{:S(2)}, u32[]{:S(2)}) collective-permute-start(bf16[128,2048]{1,0:T(8,128)(2,1)S(1)} %copy-done.2), channel_id=1, source_target_pairs={{1,0},{2,1},{3,2},{4,3},{5,4},{6,5},{7,6},{8,7},{9,8},{10,9},{11,1... | collective-permute-start | bytes 1572872 | tf_op jit(solution)/shard_map/ppermute | solution.py:376
  90.9 21.7 %collective-permute-start.3 = (bf16[16,2048]{1,0:T(8,128)(2,1)}, bf16[16,2048]{1,0:T(8,128)(2,1)S(1)}, u32[]{:S(2)}, u32[]{:S(2)}) collective-permute-start(bf16[16,2048]{1,0:T(8,128)(2,1)} %get-tuple-element.71), channel_id=1, source_target_pairs={{0,2},{1,3},{2,4},{3,5},{4,6},{5,7},{6,8},{7,9},{8,10},{9,11},{10,... | collective-permute-start | bytes 196616 | tf_op jit(solution)/shard_map/ppermute | solution.py:376
  95.2 2.5 %copy-start.9 = (f32[128,2048]{1,0:T(8,128)S(1)}, f32[128,2048]{1,0:T(8,128)}, u32[]{:S(2)}) copy-start(f32[128,2048]{1,0:T(8,128)} %copy-done.8) | copy-start | bytes 3145732
  95.2 2.8 %copy-start.11 = (f32[144,2048]{1,0:T(8,128)S(1)}, f32[144,2048]{1,0:T(8,128)}, u32[]{:S(2)}) copy-start(f32[144,2048]{1,0:T(8,128)} %copy-done.10) | copy-start | bytes 3538948
  95.3 3.1 %copy-start.15 = (bf16[256,2048]{1,0:T(8,128)(2,1)S(1)}, bf16[256,2048]{1,0:T(8,128)(2,1)}, u32[]{:S(2)}) copy-start(bf16[256,2048]{1,0:T(8,128)(2,1)} %copy-done.14) | copy-start | bytes 3145732
  97.8 13.7 %copy-start.18 = (f32[16,3840]{0,1:T(8,128)}, f32[16,3840]{0,1:T(8,128)S(1)}, u32[]{:S(2)}) copy-start(f32[16,3840]{0,1:T(8,128)S(1)} %fusion) | copy-start | bytes 737284
  111.7 0.9 slice-start
  112.3 4.2 %copy-start.20 = (bf16[2,1,128,2048]{3,2,1,0:T(8,128)(2,1)S(1)}, bf16[2,1,128,2048]{3,2,1,0:T(8,128)(2,1)}, u32[]{:S(2)}) copy-start(bf16[2,1,128,2048]{3,2,1,0:T(8,128)(2,1)} %param.8) | copy-start | bytes 3145732
  112.6 27.8 %collective-permute-start.2 = (bf16[16,2048]{1,0:T(8,128)(2,1)S(1)}, bf16[16,2048]{1,0:T(8,128)(2,1)S(1)}, u32[]{:S(2)}, u32[]{:S(2)}) collective-permute-start(bf16[16,2048]{1,0:T(8,128)(2,1)S(1)} %slice.89), channel_id=1, source_target_pairs={{2,16},{3,17},{4,18},{5,19},{6,20},{7,21},{8,22},{9,23},{10,24},{1... | collective-permute-start | bytes 196616 | tf_op jit(solution)/shard_map/ppermute | solution.py:386
  114.0 7.6 %collective-permute-start.6 = (bf16[16,2048]{1,0:T(8,128)(2,1)}, bf16[16,2048]{1,0:T(8,128)(2,1)S(1)}, u32[]{:S(2)}, u32[]{:S(2)}) collective-permute-start(bf16[16,2048]{1,0:T(8,128)(2,1)} %get-tuple-element.70), channel_id=1, source_target_pairs={{2,0},{3,1},{4,2},{5,3},{6,4},{7,5},{8,6},{9,7},{10,8},{11,9},{12,... | collective-permute-start | bytes 196616 | tf_op jit(solution)/shard_map/ppermute | solution.py:376
  121.6 1.2 copy-start.21
  137.1 1.1 copy-start.5
  138.1 1.0 copy-start.12
  139.2 1.0 copy-start.16
  140.3 1.6 copy-start.6
  141.9 15.3 %copy-start.13 = (f32[144,2048]{1,0:T(8,128)S(1)}, f32[144,2048]{1,0:T(8,128)}, u32[]{:S(2)}) copy-start(f32[144,2048]{1,0:T(8,128)} %copy-done.12) | copy-start | bytes 3538948
  141.9 15.3 %copy-start.17 = (bf16[256,2048]{1,0:T(8,128)(2,1)S(1)}, bf16[256,2048]{1,0:T(8,128)(2,1)}, u32[]{:S(2)}) copy-start(bf16[256,2048]{1,0:T(8,128)(2,1)} %copy-done.16) | copy-start | bytes 3145732

commit v3 on v2

--- a/solution.py
+++ b/solution.py
@@ -157,24 +157,6 @@
 BRANCH_SPEC = pl.BlockSpec((3, TAPS, LANES), lambda i: (0, 0, i))
 
 
-def run_forward(x_ext, r_ext, gain, short, table):
-    total, channels = x_ext.shape
-    own = TAPS + EDGE
-    shapes = [
-        ((TAPS + own), F32), (own, F32), (own, F32), (own, F32), (2 * TAPS, BF16), (own, F32),
-    ]
-    return pl.pallas_call(
-        forward_kernel,
-        grid=(channels // LANES,),
-        in_specs=[tall(total), whole((total, 1)), tall(1), tall(24), GROUP_SPEC],
-        out_specs=[tall(rows) for rows, _ in shapes],
-        out_shape=[jax.ShapeDtypeStruct((rows, channels), kind) for rows, kind in shapes],
-        scratch_shapes=[pltpu.VMEM((total, LANES), F32), pltpu.VMEM((3 * TAPS, LANES), BF16)],
-        compiler_params=pltpu.CompilerParams(**PARAMS),
-        cost_estimate=pl.CostEstimate(flops=4 * 10**9, bytes_accessed=12 * 10**6, transcendentals=0),
-    )(x_ext, r_ext, gain, short, table)
-
-
 def run_backward(e_ext, q, k, v, g, x, r, gain, short, table):
     channels = x.shape[1]
     own = TAPS + EDGE
@@ -236,17 +218,15 @@
 
 
 def start_kernel(
-    count, flat_ref, x_ref, e_ref, every_ref, xe_ref, ee_ref, send, recv, halo_send, halo_recv
+    count, flat_ref, x_ref, every_ref, xe_ref, send, recv, halo_send, halo_recv
 ):
     me = lax.axis_index("fsdp")
     rows = x_ref.shape[0]
     halos = (
         (x_ref, 0, rows, xe_ref, EDGE, 1),
-        (e_ref, 0, rows, ee_ref, rows, -1),
         (x_ref, 0, rows, xe_ref, EDGE + 2 * rows, -1),
         (x_ref, rows - EDGE, EDGE, xe_ref, 0, 2),
         (x_ref, 0, EDGE, xe_ref, EDGE + 3 * rows, -2),
-        (e_ref, 0, EDGE, ee_ref, 2 * rows, -2),
     )
 
     def halo(i, target):
@@ -286,7 +266,6 @@
 
     every_ref[me] = flat_ref[...]
     xe_ref[EDGE + rows : EDGE + 2 * rows] = x_ref[...]
-    ee_ref[:rows] = e_ref[...]
     for i, (_, _, size, landing, place, steps) in enumerate(halos):
 
         @pl.when(sends(-steps))
@@ -338,22 +317,21 @@
     lax.fori_loop(1, count, finish, 0)
 
 
-def run_start(flat, x, e, shards):
+def run_start(flat, x, shards):
     rows, channels = x.shape
     vmem = pl.BlockSpec(memory_space=pltpu.VMEM)
     dma = pltpu.SemaphoreType.DMA
     return pl.pallas_call(
         lambda *refs: start_kernel(shards, *refs),
-        in_specs=[vmem] * 3,
-        out_specs=[vmem] * 3,
+        in_specs=[vmem] * 2,
+        out_specs=[vmem] * 2,
         out_shape=[
             jax.ShapeDtypeStruct((shards,) + flat.shape, F32),
             jax.ShapeDtypeStruct((3 * rows + 2 * EDGE, channels), BF16),
-            jax.ShapeDtypeStruct((2 * rows + EDGE, channels), BF16),
-        ],
-        scratch_shapes=[dma((shards,)), dma((shards,)), dma((6,)), dma((6,))],
+        ],
+        scratch_shapes=[dma((shards,)), dma((shards,)), dma((4,)), dma((4,))],
         compiler_params=pltpu.CompilerParams(collective_id=0, has_side_effects=True, **PARAMS),
-    )(flat, x, e)
+    )(flat, x)
 
 
 def run_scatter(packed):
@@ -370,20 +348,197 @@
     )(packed)
 
 
-def shifted(value, steps):
-    count = lax.axis_size("fsdp")
-    initial, last = (max(0, -steps), min(count, count - steps))
-    return lax.ppermute(value, "fsdp", [(source, source + steps) for source in range(initial, last)])
-
-
-def crossed(value, steps):
-    sections, count = lax.axis_size("section"), lax.axis_size("fsdp")
-    pairs = [
-        (s * count + f, ((s - 1) % sections) * count + f - steps)
-        for s in range(sections)
-        for f in range(steps, count)
-    ]
-    return lax.ppermute(value, ("section", "fsdp"), pairs)
+def exchange_parts(sections, count, moves, owned, zeros, send, recv, local):
+    section, me = lax.axis_index("section"), lax.axis_index("fsdp")
+
+    def device(dsection, steps):
+        return {"section": lax.rem(section + dsection + sections, sections), "fsdp": me + steps}
+
+    def copy(i):
+        source, first, size, landing, place, dsection, steps = moves[i]
+        return pltpu.make_async_remote_copy(
+            src_ref=source.at[pl.ds(first, size)],
+            dst_ref=landing.at[pl.ds(place, size)],
+            send_sem=send.at[i],
+            recv_sem=recv.at[i],
+            device_id=device(dsection, steps),
+        )
+
+    def keep(i):
+        source, landing, place = owned[i]
+        return pltpu.make_async_copy(
+            source, landing.at[pl.ds(place, source.shape[0])], local.at[i]
+        )
+
+    def inside(steps):
+        return (me + steps >= 0) & (me + steps < count)
+
+    routes = sorted({move[5:] for move in moves})
+
+    def begin():
+        barrier = pltpu.get_barrier_semaphore()
+        for dsection, steps in routes:
+
+            @pl.when(inside(-steps))
+            def _(dsection=dsection, steps=steps):
+                pl.semaphore_signal(barrier, inc=1, device_id=device(-dsection, -steps))
+
+        pl.semaphore_wait(barrier, sum(inside(steps).astype(jnp.int32) for _, steps in routes))
+        for i, move in enumerate(moves):
+
+            @pl.when(inside(move[6]))
+            def _(i=i):
+                copy(i).start()
+
+        for i in range(len(owned)):
+            keep(i).start()
+        zeros[...] = jnp.zeros_like(zeros)
+        for i, (_, _, size, landing, place, _, steps) in enumerate(moves):
+
+            @pl.when(jnp.logical_not(inside(-steps)))
+            def _(size=size, landing=landing, place=place):
+                clear = pltpu.make_async_copy(
+                    zeros.at[pl.ds(0, size)],
+                    landing.at[pl.ds(place, size)],
+                    local.at[len(owned)],
+                )
+                clear.start()
+                clear.wait()
+
+    def finish():
+        for i, move in enumerate(moves):
+
+            @pl.when(inside(-move[6]))
+            def _(i=i):
+                copy(i).wait_recv()
+
+            @pl.when(inside(move[6]))
+            def _(i=i):
+                copy(i).wait_send()
+
+        for i in range(len(owned)):
+            keep(i).wait()
+
+    return begin, finish
+
+
+def around(begin, finish, body):
+    step = pl.program_id(0)
+    pl.when(step == 0)(begin)
+    body()
+    pl.when(step == pl.num_programs(0) - 1)(finish)
+
+
+def first_forward_kernel(
+    sections, count, x_ref, r_ref, gain_ref, short_ref, table_ref, y_ref, e_ref,
+    q_ref, k_ref, v_ref, u_ref, w_ref, g_ref, ye_ref, ee_ref, us, ws, zeros, send, recv, local,
+):
+    rows = y_ref.shape[0]
+    moves = (
+        (e_ref, 0, rows, ee_ref, rows, 0, -1),
+        (e_ref, 0, EDGE, ee_ref, 2 * rows, 0, -2),
+        (y_ref, 0, rows, ye_ref, EDGE, 0, 1),
+        (y_ref, 0, rows, ye_ref, EDGE + 2 * rows, 0, -1),
+        (y_ref, rows - EDGE, EDGE, ye_ref, 0, 0, 2),
+        (y_ref, 0, EDGE, ye_ref, EDGE + 3 * rows, 0, -2),
+    )
+    owned = ((e_ref, ee_ref, 0), (y_ref, ye_ref, EDGE + rows))
+    begin, finish = exchange_parts(sections, count, moves, owned, zeros, send, recv, local)
+    around(
+        begin,
+        finish,
+        lambda: forward_kernel(
+            x_ref, r_ref, gain_ref, short_ref, table_ref,
+            q_ref, k_ref, v_ref, u_ref, w_ref, g_ref, us, ws,
+        ),
+    )
+
+
+def middle_kernel(sections, count, *refs):
+    forward_in, terms_in, d_ref = refs[:5], refs[5:12], refs[12]
+    forward_out, terms_out, ee_ref = refs[13:19], refs[19:22], refs[22]
+    us, ws, zeros, send, recv, local = refs[23:]
+    rows = d_ref.shape[0]
+    moves = (
+        (d_ref, 0, rows, ee_ref, 0, -1, 0),
+        (d_ref, 0, rows, ee_ref, rows, -1, -1),
+        (d_ref, 0, EDGE, ee_ref, 2 * rows, -1, -2),
+    )
+    begin, finish = exchange_parts(sections, count, moves, (), zeros, send, recv, local)
+
+    def body():
+        forward_kernel(*forward_in, *forward_out, us, ws)
+        terms_kernel(*terms_in, *terms_out)
+
+    around(begin, finish, body)
+
+
+def forward_specs(total, channels):
+    own = TAPS + EDGE
+    shapes = [(TAPS + own, F32), (own, F32), (own, F32), (own, F32), (2 * TAPS, BF16), (own, F32)]
+    return (
+        [tall(total), whole((total, 1)), tall(1), tall(24), GROUP_SPEC],
+        [tall(rows) for rows, _ in shapes],
+        [jax.ShapeDtypeStruct((rows, channels), kind) for rows, kind in shapes],
+        [pltpu.VMEM((total, LANES), F32), pltpu.VMEM((3 * TAPS, LANES), BF16)],
+    )
+
+
+def terms_specs(channels):
+    return (
+        [
+            tall(TAPS), BRANCH_SPEC, tall(TAPS), tall(TAPS + EDGE), tall(2 * TAPS), tall(TAPS),
+            whole((TAPS, 1)),
+        ],
+        [tall(1), tall(24), GROUP_SPEC],
+        [
+            jax.ShapeDtypeStruct((1, channels), F32),
+            jax.ShapeDtypeStruct((24, channels), F32),
+            jax.ShapeDtypeStruct((channels // CH_GROUP, 2 * TAPS), F32),
+        ],
+    )
+
+
+def exchange_scratch(moves, owned, rows, channels):
+    dma = pltpu.SemaphoreType.DMA
+    return [pltpu.VMEM((rows, channels), BF16), dma((moves,)), dma((moves,)), dma((owned + 1,))]
+
+
+def run_first_forward(forward_args, y, e, sections, count):
+    rows, channels = y.shape
+    ins, outs, shapes, scratch = forward_specs(forward_args[0].shape[0], channels)
+    remote = pl.BlockSpec(memory_space=pl.ANY)
+    return pl.pallas_call(
+        lambda *refs: first_forward_kernel(sections, count, *refs),
+        grid=(channels // LANES,),
+        in_specs=ins + [remote] * 2,
+        out_specs=outs + [remote] * 2,
+        out_shape=shapes
+        + [
+            jax.ShapeDtypeStruct((3 * rows + 2 * EDGE, channels), BF16),
+            jax.ShapeDtypeStruct((2 * rows + EDGE, channels), BF16),
+        ],
+        scratch_shapes=scratch + exchange_scratch(6, 2, rows, channels),
+        compiler_params=pltpu.CompilerParams(collective_id=2, has_side_effects=True, **PARAMS),
+    )(*forward_args, y, e)
+
+
+def run_middle(forward_args, terms_args, d, sections, count):
+    rows, channels = d.shape
+    ins, outs, shapes, scratch = forward_specs(forward_args[0].shape[0], channels)
+    more_ins, more_outs, more_shapes = terms_specs(channels)
+    remote = pl.BlockSpec(memory_space=pl.ANY)
+    return pl.pallas_call(
+        lambda *refs: middle_kernel(sections, count, *refs),
+        grid=(channels // LANES,),
+        in_specs=ins + more_ins + [remote],
+        out_specs=outs + more_outs + [remote],
+        out_shape=shapes
+        + more_shapes
+        + [jax.ShapeDtypeStruct((2 * rows + EDGE, channels), BF16)],
+        scratch_shapes=scratch + exchange_scratch(3, 0, rows, channels),
+        compiler_params=pltpu.CompilerParams(collective_id=3, has_side_effects=True, **PARAMS),
+    )(*forward_args, *terms_args, d)
 
 
 def on_device(
@@ -403,7 +558,7 @@
     extent = flat.shape[1]
     room = -(-extent // 1024) * 1024
     flat = jnp.pad(flat, ((0, 0), (0, room - extent))).reshape(-1, LANES)
-    every, x1_ext, e1_ext = run_start(flat, x1, e1, shards)
+    every, x1_ext = run_start(flat, x1, shards)
     every = every.reshape(shards, 2, room)[:, :, :extent]
 
     def layer_params(part):
@@ -423,39 +578,35 @@
     upper = every[:, 0]
     params = (layer_params(upper), layer_params(jnp.where(last_section, every[:, 1], upper)))
 
-    def extended(x):
-        rows = x.shape[0]
-        return jnp.concatenate(
-            [
-                shifted(x[rows - EDGE :], 2), shifted(x, 1), x, shifted(x, -1),
-                shifted(x[:EDGE], -2),
-            ]
-        )
-
     def row_scale(x_ext):
         wide = x_ext.astype(F32)
         return lax.rsqrt(jnp.mean(wide * wide, axis=-1, keepdims=True) + NORM_EPS)
 
-    def terms_of(x, r, ahead, back):
-        return run_terms(back[1], back[2], back[3], ahead[3], ahead[4], x, r)
-
-    x2_ext = extended(x2)
-    r1_ext, r2_ext = row_scale(x1_ext), row_scale(x2_ext)
     own_rows = slice(TAPS + EDGE, 2 * TAPS + EDGE)
-    r1, r2 = r1_ext[own_rows], r2_ext[own_rows]
     (gain1, short1, causal1, anti1), (gain2, short2, causal2, anti2) = params
-    ahead1 = run_forward(x1_ext, r1_ext, gain1, short1, causal1)
-    back1 = run_backward(
+    sections = lax.axis_size("section")
+    r1_ext = row_scale(x1_ext)
+    r1 = r1_ext[own_rows]
+    *ahead1, x2_ext, e1_ext = run_first_forward(
+        (x1_ext, r1_ext, gain1, short1, causal1), x2, e1, sections, shards
+    )
+    r2_ext = row_scale(x2_ext)
+    r2 = r2_ext[own_rows]
+    dx1, *back1 = run_backward(
         e1_ext, ahead1[0], ahead1[1], ahead1[2], ahead1[5], x1, r1, gain1, short1, anti1
     )
-    dx1 = back1[0]
-    e2_ext = jnp.concatenate([crossed(dx1, 0), crossed(dx1, 1), crossed(dx1[:EDGE], 2)])
-    ahead2 = run_forward(x2_ext, r2_ext, gain2, short2, causal2)
-    terms1 = terms_of(x1, r1, ahead1, back1)
-    back2 = run_backward(
+    middle = run_middle(
+        (x2_ext, r2_ext, gain2, short2, causal2),
+        (*back1, ahead1[3], ahead1[4], x1, r1),
+        dx1,
+        sections,
+        shards,
+    )
+    ahead2, terms1, e2_ext = middle[:6], middle[6:9], middle[9]
+    dx2, *back2 = run_backward(
         e2_ext, ahead2[0], ahead2[1], ahead2[2], ahead2[5], x2, r2, gain2, short2, anti2
     )
-    terms2 = terms_of(x2, r2, ahead2, back2)
+    terms2 = run_terms(*back2, ahead2[3], ahead2[4], x2, r2)
     keep = jnp.where(last_section, 0.0, 1.0)
     tg, ts, tm = [a + keep * b for a, b in zip(terms1, terms2)]
     ts = jnp.transpose(ts[: 3 * SHORT].reshape(3 * SHORT, shards, chunk), (1, 0, 2))
@@ -471,7 +622,7 @@
     packed = jnp.pad(packed, ((0, 0), (0, room - width))).reshape(shards, -1, LANES)
     summed = run_scatter(packed).reshape(-1) * factor
     return (
-        back2[0][None],
+        dx2[None],
         summed[:chunk][None],
         summed[chunk : 22 * chunk].reshape(1, 3, SHORT, chunk),
         summed[22 * chunk : 30 * chunk].reshape(1, groups, TAPS // shards),

time: 188 us -> 183 us (0.973)
  starting transfers between devices: 16.1 us -> 0 us
  local copies, waits for them, and re-layouts: 27.9 us -> 34.4 us
  other arithmetic: 5.06 us -> 10.8 us
  waiting for transfers between devices: 4.04 us -> 0 us
  Pallas kernels: 131 us -> 134 us
    pallas_call x2, Pallas kernels: 28.3 us -> 55.2 us  [the longest x1 29.8 us: run_middle(): pl.pallas_call(lambda *refs: middle_kernel(sections, count, *refs), grid=...]
    ppermute x7 -> x0, starting transfers between devices: 16.1 us -> none  [the longest x4 11.5 us: shifted(): lax.ppermute(value, 'fsdp', [(source, source + steps) for source in range...]
    pallas_call x2 -> x1, Pallas kernels: 25.9 us -> 12.9 us  [run_terms(): pl.pallas_call(terms_kernel, grid=(channels // LANES,), in_specs=[tall(TA...]
    pallas_call x1, Pallas kernels: 33.4 us -> 26.4 us  [run_start(): pl.pallas_call(lambda *refs: start_kernel(shards, *refs), in_specs=[vmem]...]
    ppermute x7 -> x0, waiting for transfers between devices: 4.04 us -> none  [the longest x4 4.03 us: shifted(): lax.ppermute(value, 'fsdp', [(source, source + steps) for source in range...]
    slice x2, local copies, waits for them, and re-layouts: 1.41 us -> 5.17 us  [layer_params(): part[:, chunk:22 * chunk].reshape(shards, 3 * SHORT, chunk)]
    pallas_call x1, Pallas kernels: 11.9 us -> 9.16 us  [run_scatter(): pl.pallas_call(lambda *refs: scatter_kernel(shards, *refs), in_specs=[vme...]
    convert_element_type x2, other arithmetic: 0.07 us -> 2.19 us  [layer_params(): medium = medium.astype(BF16).astype(F32)]
  transfers between devices with their start and end apart: 7 -> 0, of which waited for: 1 -> 0; matrix products, arithmetic and copies ran while one was open for 4% -> 0% of each run, Pallas kernels for 15% -> 0%
where the time goes in v3:
time: 183 us; the launch traced here: 180 us
  Pallas kernels  134 us (73%)
  local copies, waits for them, and re-layouts  34.4 us (19%)
  other arithmetic  10.8 us (6%)
    pallas_call x2, Pallas kernels, run_backward(): pl.pallas_call(backward_kernel, grid=(blocks,), in_specs=[tall(TAPS + own...  30.6 us
    pallas_call x1, Pallas kernels, run_middle(): pl.pallas_call(lambda *refs: middle_kernel(sections, count, *refs), grid=...  29.8 us
    pallas_call x1, Pallas kernels, run_start(): pl.pallas_call(lambda *refs: start_kernel(shards, *refs), in_specs=[vmem]...  26.4 us
    pallas_call x1, Pallas kernels, run_first_forward(): pl.pallas_call(lambda *refs: first_forward_kernel(sections, count, *refs)...  25.3 us
    pallas_call x1, Pallas kernels, run_terms(): pl.pallas_call(terms_kernel, grid=(channels // LANES,), in_specs=[tall(TA...  12.9 us
    unnamed x38, local copies, waits for them, and re-layouts  12 us
    pallas_call x1, Pallas kernels, run_scatter(): pl.pallas_call(lambda *refs: scatter_kernel(shards, *refs), in_specs=[vme...  9.16 us
    slice x2, local copies, waits for them, and re-layouts, layer_params(): part[:, chunk:22 * chunk].reshape(shards, 3 * SHORT, chunk)  5.17 us

profile of v3, /device:TPU:1, one launch (start us, length us, event | category | flops | bytes accessed | tf_op | source)
XLA Modules:
  0.0 180.5 jit_solution(16504442284038716294)
XLA Ops:
  0.6 0.8 copy.25
  1.4 0.1 reshape.144
  1.5 0.7 reshape.143
  2.2 0.7 pad_maximum_fusion.1
  2.9 0.8 copy.24
  3.7 0.1 reshape.142
  3.8 0.7 reduce
  4.5 0.7 pad_maximum_fusion
  5.3 1.3 slice_bitcast_fusion.2
  6.6 26.4 %shard_map.111 = (f32[16,64,128]{2,1,0:T(8,128)S(1)}, bf16[416,2048]{1,0:T(8,128)(2,1)S(1)}) custom-call(f32[64,128]{1,0:T(8,128)S(1)} %reshape.145.refs_0_, bf16[128,2048]{1,0:T(8,128)(2,1)S(1)} %get-tuple-element.75.refs_1_.xf_ref.x_ref.refs_10_), custom_call_target="tpu_custom_call" | custom-call | tf_op jit(solution)/shard_map/pallas_call | solution.py:324
  33.0 0.4 multiply_reduce_fusion.1
  33.4 0.1 copy.32.refs_1_
  33.5 2.6 %copy.52 = f32[16,64,128]{0,2,1:T(8,128)} copy(f32[16,64,128]{2,1,0:T(8,128)S(1)} %get-tuple-element.36) | data formatting | bytes 1048576 | tf_op jit(solution)/shard_map/reshape | solution.py:562
  36.2 3.0 %slice_bitcast_fusion.1 = f32[16,3840]{0,1:T(8,128)} fusion(f32[16,2,4096]{0,2,1:T(8,128)} %bitcast.76), kind=kLoop, calls=%fused_computation.4 | loop fusion | bytes 491520 | tf_op jit(solution)/shard_map/squeeze | solution.py:578
  39.1 0.8 slice.85
  40.0 2.6 %slice.86 = f32[16,2688]{0,1:T(8,128)} slice(f32[16,3840]{0,1:T(8,128)} %slice_bitcast_fusion.1), slice={[0:16], [128:2816]} | slice | bytes 344064 | tf_op jit(solution)/shard_map/slice | solution.py:567
  42.6 1.7 copy.29
  44.4 0.1 copy.57
  44.5 1.1 convert_bitcast_fusion.1
  45.6 0.2 copy.30
  45.8 0.1 copy.31
  45.9 0.1 rev.9
  46.0 0.1 pad.31.refs_4_
  46.1 25.3 %shard_map.112 = (f32[272,2048]{1,0:T(8,128)}, f32[144,2048]{1,0:T(8,128)S(1)}, f32[144,2048]{1,0:T(8,128)S(1)}, f32[144,2048]{1,0:T(8,128)}, bf16[256,2048]{1,0...) custom-call(bf16[416,2048]{1,0:T(8,128)(2,1)} %copy-done, ...), custom_call_target="tpu_custom_call" | custom-call | tf_op jit(solution)/shard_map/pallas_call | solution.py:511
  71.5 1.1 copy-done.4
  72.6 1.0 copy-done.8
  73.6 2.3 %multiply_reduce_fusion = f32[416]{0:T(512)S(1)} fusion(bf16[416,2048]{1,0:T(8,128)(2,1)} %get-tuple-element.37.refs_0_), kind=kLoop, calls=%fused_computation | loop fusion | flops 2555488 | bytes 1705600 | tf_op jit(solution)/shard_map/reduce_sum | solution.py:583
  75.9 0.1 copy.41.refs_1_
  76.0 3.6 %fusion = f32[16,3840]{0,1:T(8,128)} fusion(f32[16,2,4096]{0,2,1:T(8,128)} %bitcast.77, pred[]{:T(512)S(6)} %eq.3), kind=kLoop, calls=%fused_computation.3 | loop fusion | flops 61440 | bytes 737281 | tf_op jit(solution)/shard_map/jit(_where)/select_n | solution.py:579
  79.7 0.8 slice.89
  80.6 2.5 %slice.90 = f32[16,2688]{0,1:T(8,128)} slice(f32[16,3840]{0,1:T(8,128)} %fusion), slice={[0:16], [128:2816]} | slice | bytes 344064 | tf_op jit(solution)/shard_map/slice | solution.py:567
  83.1 1.7 copy.36
  84.9 0.1 copy.58
  85.0 1.1 convert_bitcast_fusion
  86.1 0.2 copy.37
  86.3 0.1 copy.38
  86.4 0.1 rev.10
  86.5 0.1 pad.33.refs_4_
  86.6 0.8 slice_bitcast_fusion.5
  87.3 0.1 copy.40.r_ref.refs_11_
  87.5 1.3 copy-done.3
  88.7 1.2 copy-done.9
  90.0 15.3 %shard_map.113 = (bf16[128,2048]{1,0:T(8,128)(2,1)S(1)}, bf16[128,2048]{1,0:T(8,128)(2,1)S(1)}, bf16[3,128,2048]{2,1,0:T(8,128)(2,1)}, f32[128,2048]{1,0:T(8,128)S(1)}) custom-call(bf16[272,2048]{1,0:T(8,128)(2,1)S(1)} %copy-done.9, f32[272,2048]{1,0:T(8,128)} %get-tuple-element.39.q_ref, f32[144,2048]{1,0:T(8,128)S(1)} %copy-done.3, f32[144,2048]{1,0:T(8,128)} %copy-done.4, ...), custom_call_target="tpu_custom_call" | custom-call | flops 4000000000 | bytes 12000000 | tf_op jit(solution)/shard_map/pallas_call | solution.py:164
  105.3 29.8 %shard_map.114 = (f32[272,2048]{1,0:T(8,128)}, f32[144,2048]{1,0:T(8,128)}, f32[144,2048]{1,0:T(8,128)}, f32[144,2048]{1,0:T(8,128)}, bf16[256,2048]{1,0:T(8,128...) custom-call(bf16[416,2048]{1,0:T(8,128)(2,1)} %get-tuple-element.37., ...), custom_call_target="tpu_custom_call" | custom-call | tf_op jit(solution)/shard_map/pallas_call | solution.py:531
  135.2 1.0 copy-done.11
  136.2 0.1 slice_bitcast_fusion.4
  136.3 0.1 copy.44.r_ref
  136.4 1.3 copy-done.6
  137.7 1.3 copy-done.7
  138.9 1.2 copy-done.10
  140.2 15.3 %shard_map.115 = (bf16[128,2048]{1,0:T(8,128)(2,1)}, bf16[128,2048]{1,0:T(8,128)(2,1)S(1)}, bf16[3,128,2048]{2,1,0:T(8,128)(2,1)}, f32[128,2048]{1,0:T(8,128)S(1)}) custom-call(bf16[272,2048]{1,0:T(8,128)(2,1)S(1)} %copy-done.10, f32[272,2048]{1,0:T(8,128)} %get-tuple-element.50.q_ref, f32[144,2048]{1,0:T(8,128)S(1)} %copy-done.6, ...), custom_call_target="tpu_custom_call" | custom-call | flops 4000000000 | bytes 12000000 | tf_op jit(solution)/shard_map/pallas_call | solution.py:164
  155.5 12.9 %shard_map.116 = (f32[1,2048]{1,0:T(1,128)S(1)}, f32[24,2048]{1,0:T(8,128)S(1)}, f32[128,256]{1,0:T(8,128)S(1)}) custom-call(bf16[128,2048]{1,0:T(8,128)(2,1)S(1)} %get-tuple-element.56.dg_ref, bf16[3,128,2048]{2,1,0:T(8,128)(2,1)} %get-tuple-element.57.da_ref, f32[128,2048]{1,0:T(8,128)S(1)} %get-tuple-element.58.du_ref, f32[144,2048]{1,0:T(8,128)S(1)} %copy-done.5, ...), custom_call_target="tpu_custom_call" | custom-call | flops 4000000000 | bytes 8000000 | tf_op jit(solution)/shard_map/pallas_call | solution.py:191
  168.4 0.1 slice_add_fusion.1
  168.5 0.1 rev.11
  168.6 0.1 copy.47
  168.7 0.3 copy.48
  168.9 0.2 copy.49
  169.2 0.1 copy.46
  169.4 0.1 copy.61
  169.4 9.2 %shard_map.117 = f32[32,128]{1,0:T(8,128)S(1)} custom-call(f32[16,32,128]{2,1,0:T(8,128)S(1)} %bitcast.70), custom_call_target="tpu_custom_call" | custom-call | tf_op jit(solution)/shard_map/pallas_call | solution.py:341
  178.6 0.5 slice.96
  179.1 0.6 reshape.165
  179.7 0.1 reshape.160
  179.8 0.7 copy.51
  (44 shorter events, 0.5 us)
Async XLA Ops:
  32.9 3.2 %copy-start = (bf16[416,2048]{1,0:T(8,128)(2,1)}, bf16[416,2048]{1,0:T(8,128)(2,1)S(1)}, u32[]{:S(2)}) copy-start(bf16[416,2048]{1,0:T(8,128)(2,1)S(1)} %get-tuple-element.35.refs_0_) | copy-start | bytes 5111812
  33.4 2.8 %copy-start.13 = (f32[416]{0:T(512)}, f32[416]{0:T(512)S(1)}, u32[]{:S(2)}) copy-start(f32[416]{0:T(512)S(1)} %add_rsqrt_fusion.1) | copy-start | bytes 4996
  44.4 1.8 copy-start.1
  71.5 1.1 copy-start.4
  72.6 1.0 copy-start.8
  73.6 2.3 %copy-start.2 = (f32[144,2048]{1,0:T(8,128)}, f32[144,2048]{1,0:T(8,128)S(1)}, u32[]{:S(2)}) copy-start(f32[144,2048]{1,0:T(8,128)S(1)} %get-tuple-element.40.k_ref) | copy-start | bytes 3538948
  87.5 1.3 copy-start.3
  88.7 1.2 copy-start.9
  135.2 1.0 copy-start.11
  136.4 1.3 copy-start.6
  137.7 1.3 copy-start.7
  138.9 1.2 copy-start.10
  140.2 15.3 %copy-start.5 = (f32[144,2048]{1,0:T(8,128)S(1)}, f32[144,2048]{1,0:T(8,128)}, u32[]{:S(2)}) copy-start(f32[144,2048]{1,0:T(8,128)} %get-tuple-element.59.u_ref) | copy-start | bytes 3538948
  140.2 15.3 %copy-start.12 = (bf16[256,2048]{1,0:T(8,128)(2,1)S(1)}, bf16[256,2048]{1,0:T(8,128)(2,1)}, u32[]{:S(2)}) copy-start(bf16[256,2048]{1,0:T(8,128)(2,1)} %copy-done.11) | copy-start | bytes 3145732

commit v4 on v3

--- a/solution.py
+++ b/solution.py
@@ -550,8 +550,8 @@
     channels = chunk * shards
     flat = jnp.stack(
         [
-            jnp.concatenate([gains.reshape(-1), short_filters.reshape(-1), medium_filters.reshape(-1)]),
-            jnp.concatenate([lower_gain, lower_short.reshape(-1), lower_medium.reshape(-1)]),
+            jnp.concatenate([gains.reshape(-1), short_filters.reshape(-1), medium_filters[0].T.reshape(-1)]),
+            jnp.concatenate([lower_gain, lower_short.reshape(-1), lower_medium.T.reshape(-1)]),
         ]
     )
     x1, x2, e1 = inputs[0, 0], inputs[1, 0], top_grad[0]
@@ -559,16 +559,20 @@
     room = -(-extent // 1024) * 1024
     flat = jnp.pad(flat, ((0, 0), (0, room - extent))).reshape(-1, LANES)
     every, x1_ext = run_start(flat, x1, shards)
-    every = every.reshape(shards, 2, room)[:, :, :extent]
+    by_rows = chunk == LANES
+    every = every.reshape(shards, 2, room // LANES, LANES)
 
     def layer_params(part):
-        gain = part[:, :chunk].reshape(1, channels)
-        short = jnp.transpose(
-            part[:, chunk : 22 * chunk].reshape(shards, 3 * SHORT, chunk), (1, 0, 2)
-        ).reshape(3 * SHORT, channels)
-        medium = jnp.transpose(
-            part[:, 22 * chunk :].reshape(shards, -1, TAPS // shards), (1, 0, 2)
-        ).reshape(-1, TAPS)
+        if by_rows:
+            gain, short, medium = part[:, :1], part[:, 1:22], part[:, 22:30]
+        else:
+            part = part.reshape(shards, room)
+            gain, short = part[:, :chunk], part[:, chunk : 22 * chunk]
+            medium = part[:, 22 * chunk : extent]
+        gain = gain.reshape(1, channels)
+        short = jnp.transpose(short.reshape(shards, 3 * SHORT, chunk), (1, 0, 2))
+        short = short.reshape(3 * SHORT, channels)
+        medium = medium.reshape(TAPS, -1).T
         medium = medium.astype(BF16).astype(F32)
         short = jnp.pad(short, ((0, 3), (0, 0)))
         causal = jnp.pad(medium[:, ::-1], ((0, 0), (1, TAPS - 1)))
@@ -612,7 +616,7 @@
     ts = jnp.transpose(ts[: 3 * SHORT].reshape(3 * SHORT, shards, chunk), (1, 0, 2))
     tm = tm[:, 1 : TAPS + 1][:, ::-1]
     groups = tm.shape[0]
-    tm = jnp.transpose(tm.reshape(groups, shards, TAPS // shards), (1, 0, 2))
+    tm = tm.T
     packed = jnp.concatenate(
         [tg.reshape(shards, chunk), ts.reshape(shards, -1), tm.reshape(shards, -1)], axis=1
     )
@@ -625,7 +629,7 @@
         dx2[None],
         summed[:chunk][None],
         summed[chunk : 22 * chunk].reshape(1, 3, SHORT, chunk),
-        summed[22 * chunk : 30 * chunk].reshape(1, groups, TAPS // shards),
+        summed[22 * chunk : 30 * chunk].reshape(TAPS // shards, groups).T[None],
     )
 
 

time: 183 us -> 168 us (0.918)
  other arithmetic: 10.8 us -> 1.74 us
  local copies, waits for them, and re-layouts: 34.4 us -> 28.9 us
    unnamed x38 -> x69, local copies, waits for them, and re-layouts: 12 us -> 19.7 us
    slice x7 -> x0, local copies, waits for them, and re-layouts: 6.96 us -> none  [the longest x2 5.17 us: layer_params(): part[:, chunk:22 * chunk].reshape(shards, 3 * SHORT, chunk)]
    select_n x1, other arithmetic: 3.64 us -> 0.04 us  [on_device(): jnp.where(last_section, every[:, 1], upper)]
    transpose x3 -> x5, local copies, waits for them, and re-layouts: 3.69 us -> 0.21 us  [the longest x4 0.11 us: layer_params(): short = jnp.transpose(short.reshape(shards, 3 * SHORT, chunk), (1, 0, 2))]
    squeeze x1, local copies, waits for them, and re-layouts: 2.96 us -> 0.02 us  [on_device(): upper = every[:, 0]]
    reshape x4 -> x2, local copies, waits for them, and re-layouts: 2.89 us -> 0.86 us  [layer_params(): gain = gain.reshape(1, channels)]
    reduce_sum x2, other arithmetic: 2.7 us -> 0.82 us  [row_scale(): return lax.rsqrt(jnp.mean(wide * wide, axis=-1, keepdims=True) + NORM_EPS)]
where the time goes in v4:
time: 168 us; the launch traced here: 166 us
  Pallas kernels  134 us (80%)
  local copies, waits for them, and re-layouts  28.9 us (17%)
  other arithmetic  1.74 us (1%)
    pallas_call x2, Pallas kernels, run_backward(): pl.pallas_call(backward_kernel, grid=(blocks,), in_specs=[tall(TAPS + own...  30.8 us
    pallas_call x1, Pallas kernels, run_middle(): pl.pallas_call(lambda *refs: middle_kernel(sections, count, *refs), grid=...  29.9 us
    pallas_call x1, Pallas kernels, run_start(): pl.pallas_call(lambda *refs: start_kernel(shards, *refs), in_specs=[vmem]...  26.4 us
    pallas_call x1, Pallas kernels, run_first_forward(): pl.pallas_call(lambda *refs: first_forward_kernel(sections, count, *refs)...  25.3 us
    unnamed x69, local copies, waits for them, and re-layouts  19.7 us
    pallas_call x1, Pallas kernels, run_terms(): pl.pallas_call(terms_kernel, grid=(channels // LANES,), in_specs=[tall(TA...  12.9 us
    pallas_call x1, Pallas kernels, run_scatter(): pl.pallas_call(lambda *refs: scatter_kernel(shards, *refs), in_specs=[vme...  9.12 us

profile of v4, /device:TPU:1, one launch (start us, length us, event | category | flops | bytes accessed | tf_op | source)
XLA Modules:
  0.0 166.2 jit_solution(5314718408531297911)
XLA Ops:
  0.6 0.0 copy-start.26
  0.6 0.0 copy-start.29
  0.7 0.0 copy-start.27
  0.7 1.3 slice_bitcast_fusion
  2.1 0.0 copy-done.25
  2.3 26.4 %shard_map.111 = (f32[16,64,128]{2,1,0:T(8,128)S(1)}, bf16[416,2048]{1,0:T(8,128)(2,1)S(1)}) custom-call(f32[64,128]{1,0:T(8,128)S(1)} %reshape.125.refs_0_, bf16[128,2048]{1,0:T(8,128)(2,1)S(1)} %get-tuple-element.75.refs_1_.xf_ref.x_ref.refs_10_), custom_call_target="tpu_custom_call" | custom-call | tf_op jit(solution)/shard_map/pallas_call | solution.py:324
  28.7 0.0 copy-start.24
  28.8 0.1 copy.41
  28.9 0.6 copy-done.24
  29.5 0.6 fusion.3
  30.1 0.9 copy.26
  31.0 0.7 rev.9
  31.7 1.6 pad.31.refs_4_
  33.3 0.8 slice_bitcast_fusion.7.refs_2_.gain_ref
  34.2 0.4 multiply_reduce_fusion.1
  34.6 0.1 copy.27.refs_1_
  34.7 0.0 copy-start.3
  34.8 1.0 copy-done.3
  35.8 0.9 copy-done.8
  36.7 25.3 %shard_map.112 = (f32[272,2048]{1,0:T(8,128)}, f32[144,2048]{1,0:T(8,128)S(1)}, f32[144,2048]{1,0:T(8,128)S(1)}, f32[144,2048]{1,0:T(8,128)}, bf16[256,2048]{1,0...) custom-call(bf16[416,2048]{1,0:T(8,128)(2,1)} %copy-done, ...), custom_call_target="tpu_custom_call" | custom-call | tf_op jit(solution)/shard_map/pallas_call | solution.py:511
  62.0 1.0 copy-done.15
  63.0 1.0 copy-done.17
  64.1 1.0 copy-done.19
  65.1 0.7 pad.34.table_ref
  65.7 0.1 slice_bitcast_fusion.10
  65.8 0.1 copy.31.r_ref.refs_11_
  65.9 0.9 copy-done.9
  66.8 1.3 copy-done.16
  68.1 1.2 copy-done.20
  69.3 15.4 %shard_map.113 = (bf16[128,2048]{1,0:T(8,128)(2,1)S(1)}, bf16[128,2048]{1,0:T(8,128)(2,1)S(1)}, bf16[3,128,2048]{2,1,0:T(8,128)(2,1)}, f32[128,2048]{1,0:T(8,128)S(1)}) custom-call(bf16[272,2048]{1,0:T(8,128)(2,1)S(1)} %copy-done.20, f32[272,2048]{1,0:T(8,128)} %get-tuple-element.39.q_ref, f32[144,2048]{1,0:T(8,128)S(1)} %copy-done.16, ...), custom_call_target="tpu_custom_call" | custom-call | flops 4000000000 | bytes 12000000 | tf_op jit(solution)/shard_map/pallas_call | solution.py:164
  84.8 1.0 copy-done.1
  85.8 0.0 copy-done.23
  85.8 0.4 multiply_reduce_fusion
  86.2 0.4 copy-done.4
  86.6 0.2 copy-done.6
  86.7 0.1 copy.32.refs_1_
  87.0 0.1 copy.42
  87.2 0.1 copy.30
  87.3 0.1 rev.10
  87.3 0.1 pad.33.refs_4_
  87.5 0.5 copy-done.5
  88.0 1.2 copy-done.2
  89.2 1.0 copy-done.7
  90.2 29.9 %shard_map.114 = (f32[272,2048]{1,0:T(8,128)}, f32[144,2048]{1,0:T(8,128)}, f32[144,2048]{1,0:T(8,128)}, f32[144,2048]{1,0:T(8,128)}, bf16[256,2048]{1,0:T(8,128...) custom-call(bf16[416,2048]{1,0:T(8,128)(2,1)} %get-tuple-element.37., ...), custom_call_target="tpu_custom_call" | custom-call | tf_op jit(solution)/shard_map/pallas_call | solution.py:531
  120.1 0.6 copy-done.10
  120.8 1.0 copy-done.21
  121.7 0.1 slice_bitcast_fusion.9
  121.8 0.1 copy.34.r_ref
  122.0 1.3 copy-done.13
  123.2 1.3 copy-done.14
  124.5 1.2 copy-done.18
  125.7 15.3 %shard_map.115 = (bf16[128,2048]{1,0:T(8,128)(2,1)}, bf16[128,2048]{1,0:T(8,128)(2,1)S(1)}, bf16[3,128,2048]{2,1,0:T(8,128)(2,1)}, f32[128,2048]{1,0:T(8,128)S(1)}) custom-call(bf16[272,2048]{1,0:T(8,128)(2,1)S(1)} %copy-done.18, f32[272,2048]{1,0:T(8,128)} %get-tuple-element.50.q_ref, f32[144,2048]{1,0:T(8,128)S(1)} %copy-done.13, ...), custom_call_target="tpu_custom_call" | custom-call | flops 4000000000 | bytes 12000000 | tf_op jit(solution)/shard_map/pallas_call | solution.py:164
  141.1 0.0 copy-done.12
  141.1 12.9 %shard_map.116 = (f32[1,2048]{1,0:T(1,128)S(1)}, f32[24,2048]{1,0:T(8,128)S(1)}, f32[128,256]{1,0:T(8,128)S(1)}) custom-call(bf16[128,2048]{1,0:T(8,128)(2,1)S(1)} %get-tuple-element.56.dg_ref, bf16[3,128,2048]{2,1,0:T(8,128)(2,1)} %get-tuple-element.57.da_ref, f32[128,2048]{1,0:T(8,128)S(1)} %get-tuple-element.58.du_ref, f32[144,2048]{1,0:T(8,128)S(1)} %copy-done.12, ...), custom_call_target="tpu_custom_call" | custom-call | flops 4000000000 | bytes 8000000 | tf_op jit(solution)/shard_map/pallas_call | solution.py:191
  154.1 0.1 copy.36
  154.2 0.7 copy-done.11
  154.9 0.1 slice_add_fusion.1
  155.0 0.1 rev.11
  155.1 0.1 copy.37
  155.2 0.1 copy.45
  155.3 9.1 %shard_map.117 = f32[32,128]{1,0:T(8,128)S(1)} custom-call(f32[16,32,128]{2,1,0:T(8,128)S(1)} %bitcast.79), custom_call_target="tpu_custom_call" | custom-call | tf_op jit(solution)/shard_map/pallas_call | solution.py:341
  164.4 0.6 reshape.139
  165.1 0.6 slice_bitcast_fusion.8
  165.6 0.5 slice.93
  (66 shorter events, 0.6 us)
Async XLA Ops:
  0.6 1.4 copy-start.26
  0.6 1.4 copy-start.29
  0.7 1.4 copy-start.27
  0.7 1.5 copy-start.25
  0.7 1.5 copy-start.28
  0.7 1.5 copy-start.30
  28.6 5.9 %copy-start = (bf16[416,2048]{1,0:T(8,128)(2,1)}, bf16[416,2048]{1,0:T(8,128)(2,1)S(1)}, u32[]{:S(2)}) copy-start(bf16[416,2048]{1,0:T(8,128)(2,1)S(1)} %get-tuple-element.35.refs_0_) | copy-start | bytes 5111812
  28.7 0.8 copy-start.24
  34.7 1.0 copy-start.3
  35.8 0.9 copy-start.8
  62.0 1.0 copy-start.15
  63.0 1.0 copy-start.17
  64.1 1.0 copy-start.19
  65.9 0.9 copy-start.9
  66.8 1.3 copy-start.16
  68.1 1.2 copy-start.20
  69.3 16.4 %copy-start.23 = (bf16[416,2048]{1,0:T(8,128)(2,1)S(1)}, bf16[416,2048]{1,0:T(8,128)(2,1)}, u32[]{:S(2)}) copy-start(bf16[416,2048]{1,0:T(8,128)(2,1)} %get-tuple-element.37.refs_0_) | copy-start | bytes 5111812
  84.8 1.0 copy-start.1
  85.8 0.8 copy-start.4
  85.8 1.0 copy-start.6
  86.9 1.0 copy-start.5
  88.0 1.2 copy-start.2
  89.2 1.0 copy-start.7
  120.1 0.7 copy-start.10
  120.8 1.0 copy-start.21
  121.9 1.3 copy-start.13
  123.2 1.3 copy-start.14
  124.5 1.2 copy-start.18
  125.7 15.3 %copy-start.12 = (f32[144,2048]{1,0:T(8,128)S(1)}, f32[144,2048]{1,0:T(8,128)}, u32[]{:S(2)}) copy-start(f32[144,2048]{1,0:T(8,128)} %get-tuple-element.59.u_ref) | copy-start | bytes 3538948
  125.7 15.3 %copy-start.22 = (bf16[256,2048]{1,0:T(8,128)(2,1)S(1)}, bf16[256,2048]{1,0:T(8,128)(2,1)}, u32[]{:S(2)}) copy-start(bf16[256,2048]{1,0:T(8,128)(2,1)} %copy-done.21) | copy-start | bytes 3145732
  154.0 0.9 copy-start.11
